TPU v7x, 256 devices: a whole 4x4x8 slice. The times are simulated.
256 devices in a mesh: section: 4 (over y_lo, core), tensor: 8 (over z), dp: 8 (over y_hi, x).
Axes of the slice: x: 4, y: 4 (y_hi: 2, y_lo: 2; y = y_hi * 2 + y_lo), z: 8, core: 2. Of those that a mesh axis runs over, the one named last changes fastest.
Arguments:
- x_in: bfloat16 [1, 1024, 2048], P(None, 'dp', ('section', 'tensor')), may hold values from -40 to 40
- gate_weight: bfloat16 [4, 2048, 7168], P('section', None, 'tensor'), may hold values from -0.125 to 0.125
- up_weight: bfloat16 [4, 2048, 7168], P('section', None, 'tensor'), may hold values from -0.125 to 0.125
- down_weight: bfloat16 [4, 7168, 2048], P('section', 'tensor'), may hold values from -0.0625 to 0.0625
- norm_gain: float32 [4, 2048], P('section'), may hold values from 0.1 to 1.9
- cotangent: bfloat16 [1, 1024, 2048], P(None, 'dp', ('section', 'tensor')), may hold values from -0.5 to 0.5
Outputs:
- new_grad: float32 [4, 7168, 2048], P('section', 'tensor', 'dp')
All inputs are finite; a program needn't handle non-finite values.
Results may differ from a plain program's by a relative error of at most 0.035.
Values may be sent and summed in bfloat16 or wider, within the bound.
A program may use at most 128 MiB of HBM per device.

v0:
```python
import jax
import jax.numpy as jnp
from jax import lax
from jax.sharding import PartitionSpec as P

EPSILON = 1e-05
CONTRACT_FIRST = (((0,), (0,)), ((), ()))


def shifted(block, axis, distance):
    devices = range(lax.axis_size(axis))
    route = [(i - distance, i) for i in devices if i - distance in devices]
    return lax.ppermute(block, axis, route)


def normalize(activations, norm_scale):
    values = activations.astype(jnp.float32)
    inv_rms = lax.rsqrt(jnp.mean(values * values, axis=-1, keepdims=True) + EPSILON)
    return (values * inv_rms * norm_scale).astype(jnp.bfloat16)


def norm_back(activations, norm_scale, incoming):
    values = activations.astype(jnp.float32)
    inv_rms = lax.rsqrt(jnp.mean(values * values, axis=-1, keepdims=True) + EPSILON)
    weighted = incoming * norm_scale
    return inv_rms * weighted - values * inv_rms * inv_rms * inv_rms * jnp.mean(
        values * weighted, axis=-1, keepdims=True
    )


def place(store, slot_index, value, active):
    previous = lax.dynamic_index_in_dim(store, slot_index, 0, keepdims=False)
    return lax.dynamic_update_index_in_dim(store, jnp.where(active, value, previous), slot_index, 0)


def tensor_total(partial_value):
    return lax.psum(partial_value.astype(jnp.bfloat16), "tensor").astype(jnp.float32)


def pass_full(activations, offset):
    return shifted(activations, "section", offset)


def shards(x_in, gate_weight, up_weight, down_weight, norm_gain, cotangent):
    section_count = lax.axis_size("section")
    section_index = lax.axis_index("section")
    gate_w = gate_weight[0]
    up_w = up_weight[0]
    down_w = down_weight[0]
    gate_back = jnp.transpose(gate_w)
    up_back = jnp.transpose(up_w)
    down_back = jnp.transpose(down_w)
    norm_scale = norm_gain[0]
    micro_count = x_in.shape[0]
    inputs, targets = (
        lax.all_gather(x_in, ("section", "tensor"), axis=2, tiled=True),
        lax.all_gather(cotangent, ("section", "tensor"), axis=2, tiled=True),
    )
    row_count = inputs.shape[1]
    feature_count = inputs.shape[2]
    hidden_count = gate_w.shape[1]

    def frozen_forward(whole_rows):
        normed = normalize(whole_rows, norm_scale)
        gate_pre = jnp.dot(normed, gate_w, preferred_element_type=jnp.float32)
        up_pre = jnp.dot(normed, up_w, preferred_element_type=jnp.float32)
        hidden = (jax.nn.silu(gate_pre) * up_pre).astype(jnp.bfloat16)
        return (jnp.dot(hidden, down_w, preferred_element_type=jnp.float32), gate_pre, up_pre)

    def frozen_spare(whole_rows):
        empty_hidden = jnp.zeros((row_count, hidden_count), jnp.float32)
        return (jnp.zeros((row_count, feature_count), jnp.float32), empty_hidden, empty_hidden)

    def expanded_forward(whole_rows):
        normed = normalize(whole_rows, norm_scale)
        gate_new = jnp.dot(normed, gate_w, preferred_element_type=jnp.float32)
        up_new = jnp.dot(normed, up_w, preferred_element_type=jnp.float32)
        return (jax.nn.silu(gate_new) * up_new).astype(jnp.bfloat16)

    def expanded_spare(whole_rows):
        return jnp.zeros((row_count, hidden_count), jnp.bfloat16)

    def frozen_backward(operands):
        incoming, gate_pre, up_pre = operands
        back_hidden = jnp.dot(incoming, down_back, preferred_element_type=jnp.float32)
        sigmoid_gate = jax.nn.sigmoid(gate_pre)
        d_up = (back_hidden * gate_pre * sigmoid_gate).astype(jnp.bfloat16)
        d_gate = (
            back_hidden * up_pre * sigmoid_gate * (1.0 + gate_pre * (1.0 - sigmoid_gate))
        ).astype(jnp.bfloat16)
        from_gate = jnp.dot(d_gate, gate_back, preferred_element_type=jnp.float32)
        return from_gate + jnp.dot(d_up, up_back, preferred_element_type=jnp.float32)

    def backward_spare(operands):
        return jnp.zeros((row_count, feature_count), jnp.float32)

    row_store = jnp.zeros((micro_count, row_count, feature_count), jnp.bfloat16)
    gate_store = jnp.zeros((micro_count, row_count, hidden_count), jnp.float32)
    up_store = jnp.zeros((micro_count, row_count, hidden_count), jnp.float32)
    expanded_store = jnp.zeros((micro_count, row_count, hidden_count), jnp.bfloat16)
    carried = jnp.zeros((row_count, feature_count), jnp.bfloat16)
    for timestep in range(micro_count + section_count - 1):
        position = timestep - section_index
        active = jnp.logical_and(position >= 0, position < micro_count)
        slot_index = jnp.clip(position, 0, micro_count - 1)
        arriving = inputs[min(timestep, micro_count - 1)]
        whole_rows = jnp.where(section_index == 0, arriving, carried)
        partial_value, gate_pre, up_pre = lax.cond(active, frozen_forward, frozen_spare, whole_rows)
        output = (whole_rows.astype(jnp.float32) + tensor_total(partial_value)).astype(jnp.bfloat16)
        carried = pass_full(output, 1)
        expanded = lax.cond(active, expanded_forward, expanded_spare, output)
        row_store = place(row_store, slot_index, whole_rows, active)
        gate_store = place(gate_store, slot_index, gate_pre, active)
        up_store = place(up_store, slot_index, up_pre, active)
        expanded_store = place(expanded_store, slot_index, expanded, active)
    accumulated = jnp.zeros((hidden_count, feature_count), jnp.float32)
    carried = jnp.zeros((row_count, feature_count), jnp.bfloat16)
    for timestep in range(micro_count + section_count - 1):
        position = timestep - (section_count - 1 - section_index)
        active = jnp.logical_and(position >= 0, position < micro_count)
        slot_index = jnp.clip(position, 0, micro_count - 1)
        arriving = targets[min(timestep, micro_count - 1)]
        is_final = section_index == section_count - 1
        incoming = jnp.where(is_final, arriving, carried)
        expanded = lax.dynamic_index_in_dim(expanded_store, slot_index, 0, keepdims=False)
        gate_pre = lax.dynamic_index_in_dim(gate_store, slot_index, 0, keepdims=False)
        up_pre = lax.dynamic_index_in_dim(up_store, slot_index, 0, keepdims=False)
        stored = lax.dynamic_index_in_dim(row_store, slot_index, 0, keepdims=False)
        accumulated = lax.cond(
            active,
            lambda summed: summed
            + lax.dot_general(
                expanded, incoming, CONTRACT_FIRST, preferred_element_type=jnp.float32
            ),
            lambda summed: summed,
            accumulated,
        )
        frozen_active = jnp.logical_and(active, section_index > 0)
        partial_value = lax.cond(
            frozen_active, frozen_backward, backward_spare, (incoming, gate_pre, up_pre)
        )
        change = norm_back(stored, norm_scale, tensor_total(partial_value))
        previous = (incoming.astype(jnp.float32) + change).astype(jnp.bfloat16)
        carried = pass_full(previous, -1)
    result = lax.psum_scatter(
        accumulated.astype(jnp.bfloat16), "dp", scatter_dimension=1, tiled=True
    ).astype(jnp.float32)
    return result[None]


def solution(mesh):
    placed = (
        P(None, "dp", ("section", "tensor")),
        P("section", None, "tensor"),
        P("section", None, "tensor"),
        P("section", "tensor", None),
        P("section", None),
        P(None, "dp", ("section", "tensor")),
    )
    return jax.shard_map(
        shards, mesh=mesh, in_specs=placed, out_specs=P("section", "tensor", "dp"), check_vma=False
    )
```

profile of v0, /device:TPU:2, one launch (start us, length us, event | category | flops | bytes accessed | tf_op | source)
XLA Modules:
  0.0 820.5 jit_solution(7646950433980018661)
XLA Ops:
  6.5 61.1 %all_gather.6 = bf16[1,128,2048]{1,2,0:T(8,128)(2,1)S(1)} all-gather(bf16[1,128,64]{1,2,0:T(8,128)(2,1)} %param.36), channel_id=1, replica_groups=mesh['section'=4,'tensor'=8,'dp'=8] {'section','tensor'}, dimensions={2}, use_global_device_ids=true | all-gather | bytes 540672 | tf_op jit(solution)/shard_map/all_gather | solution.py:56
  67.7 6.2 copy.35
  73.8 6.1 copy.36
  79.9 6.1 copy.37
  86.1 9.3 %conditional.15 = (bf16[128,2048]{1,0:T(8,128)(2,1)S(1)}, f32[128,896]{1,0:T(8,128)}, f32[128,896]{1,0:T(8,128)}) conditional(s32[]{:T(128)} %convert_element_type.226, () %tuple.105, (bf16[128,2048]{0,1:T(8,128)(2,1)S(1)}, f32[1,2048]{1,0:T(1,128)S(1)}, bf16[2048,896]{0,1:T(8,128)(2,1)}, bf16[2048,896]{0,1:T(8,128)(2,1)}, ...), branch_computations={%region_0.1_spmd, %region_1.3_spmd} | conditional | flops 1412857984 | bytes 45369936 | solution.py:108
  86.5 4.3 fusion.5
  90.8 2.1 fusion.7
  92.9 2.5 fusion.3
  96.5 70.5 %all-reduce.8.cloned.1.call-done = bf16[128,2048]{0,1:T(8,128)(2,1)} async-done(((bf16[128,2048]{0,1:T(8,128)(2,1)}), bf16[128,2048]{0,1:T(8,128)(2,1)}) %all-reduce.8.cloned.1.call-update) | async-done | bytes 524304 | tf_op jit(solution)/shard_map/psum | solution.py:37
  168.2 1.3 collective-permute-start
  169.6 1.5 collective-permute-done
  171.1 1.7 conditional.16
  173.9 85.7 %all-reduce.10.cloned.1.call-done = bf16[128,2048]{0,1:T(8,128)(2,1)} async-done(((bf16[128,2048]{0,1:T(8,128)(2,1)}), bf16[128,2048]{0,1:T(8,128)(2,1)}) %all-reduce.10.cloned.1.call-update) | async-done | bytes 524304 | tf_op jit(solution)/shard_map/psum | solution.py:37
  260.8 1.3 collective-permute-start.1
  262.1 1.5 collective-permute-done.1
  263.7 1.8 conditional.17
  266.5 86.9 %all-reduce.12.cloned.1.call-done = bf16[128,2048]{0,1:T(8,128)(2,1)} async-done(((bf16[128,2048]{0,1:T(8,128)(2,1)}), bf16[128,2048]{0,1:T(8,128)(2,1)}) %all-reduce.12.cloned.1.call-update) | async-done | bytes 524304 | tf_op jit(solution)/shard_map/psum | solution.py:37
  354.6 2.5 collective-permute-start.2
  357.1 55.8 %all_gather.7 = bf16[1,128,2048]{1,2,0:T(8,128)(2,1)S(1)} all-gather(bf16[1,128,64]{1,2,0:T(8,128)(2,1)S(1)} %copy-done.29), channel_id=1, replica_groups=mesh['section'=4,'tensor'=8,'dp'=8] {'section','tensor'}, dimensions={2}, use_global_device_ids=true | all-gather | bytes 540672 | tf_op jit(solution)/shard_map/all_gather | solution.py:57
  413.9 2.4 conditional.18
  416.3 1.4 select_select_fusion.1
  418.9 82.4 %all-reduce.14.cloned.1.call-done = bf16[128,2048]{0,1:T(8,128)(2,1)} async-done(((bf16[128,2048]{0,1:T(8,128)(2,1)}), bf16[128,2048]{0,1:T(8,128)(2,1)}) %all-reduce.14.cloned.1.call-update) | async-done | bytes 524304 | tf_op jit(solution)/shard_map/psum | solution.py:37
  501.3 1.6 fusion.85
  502.9 1.5 fusion.93
  505.7 2.5 collective-permute-done.3
  509.1 2.0 copy.75
  511.2 82.5 %all-reduce.16.cloned.1.call-done = bf16[128,2048]{0,1:T(8,128)(2,1)} async-done(((bf16[128,2048]{0,1:T(8,128)(2,1)}), bf16[128,2048]{0,1:T(8,128)(2,1)}) %all-reduce.16.cloned.1.call-update) | async-done | bytes 524304 | tf_op jit(solution)/shard_map/psum | solution.py:37
  593.7 1.4 fusion.101
  595.1 1.5 fusion.96
  598.0 2.0 copy.57
  602.7 2.1 copy.78
  604.9 8.3 %conditional.22 = (bf16[128,896]{1,0:T(8,128)(2,1)S(1)}) conditional(s32[]{:T(128)} %convert_element_type.226, () %tuple.118, (bf16[128,2048]{0,1:T(8,128)(2,1)}, f32[1,2048]{1,0:T(1,128)S(1)}, bf16[2048,896]{0,1:T(8,128)(2,1)}, bf16[2048,896]{0,1:T(8,128)(2,1)}) %tuple.245), branch_computations={%region_25.26_spmd, %region_26.28_spmd} | conditional | flops 943095936 | bytes 27904576 | solution.py:111
  604.9 2.0 copy.67
  606.9 1.4 fusion.62
  608.3 3.5 fusion.66
  611.9 1.3 fusion.61
  613.3 77.9 %all-reduce.18.cloned.1.call-done = (bf16[128,2048]{0,1:T(8,128)(2,1)}, bf16[128,2048]{0,1:T(8,128)(2,1)}) async-done(((bf16[128,2048]{0,1:T(8,128)(2,1)}, bf16[128,2048]{0,1:T(8,128)(2,1)}), (bf16[128,2048]{0,1:T(8,128)(2,1)}, bf16[128,2048]{0,1:T(8,128)(2,1)})) %all-reduce.18.cloned.1.call-update) | async-done | bytes 1048592 | tf_op jit(solution)/shard_map/psum | solution.py:37
  691.2 1.4 fusion.102
  692.6 2.3 fusion.99
  696.3 2.0 add_convert_fusion
  699.3 3.9 conditional.23
  699.3 3.9 broadcast_in_dim.32
  703.2 16.1 %conditional.29 = (bf16[896,2048]{0,1:T(8,128)(2,1)}) conditional(s32[]{:T(128)} %convert_element_type.220, (f32[896,2048]{1,0:T(8,128)}) %conditional.27, (pred[]{:T(512)}, bf16[128,2048]{0,1:T(8,128)(2,1)S(1)}, bf16[128,2048]{0,1:T(8,128)(2,1)}, bf16[128,896]{1,0:T(8,128)(2,1)S(1)}, f32[896,2048]{1,0:T(8,128)}) %tuple.232), branch_computations={%region_47.48_spmd, %region_48.49_spmd} | conditional | flops 473694208 | bytes 29065224 | solution.py:129
  703.2 8.6 %copy.82 = f32[896,2048]{0,1:T(8,128)} copy(f32[896,2048]{1,0:T(8,128)} %get-tuple-element.375) | data formatting | bytes 14680064 | tf_op jit(solution)/shard_map
  713.3 6.0 bitcast_add_fusion
  719.3 6.2 copy.83
  725.5 85.9 %reduce-scatter.2.cloned.1.call-done = bf16[896,256]{1,0:T(8,128)(2,1)} async-done(((bf16[896,2048]{1,0:T(8,128)(2,1)}), bf16[896,256]{1,0:T(8,128)(2,1)}) %reduce-scatter.2.cloned.1.call-update) | async-done | bytes 458768 | tf_op jit(solution)/shard_map/reduce_scatter | solution.py:145
  811.4 2.0 bitcast_convert_fusion
  (94 shorter events, 27.2 us)
Async XLA Ops:
  6.5 160.5 %all-reduce.8.cloned.1.call-start = ((), (), s32[]{:S(2)}) async-start(), calls=%async_computation.1 | async-start | bytes 1048576 | tf_op jit(solution)/shard_map/psum | solution.py:37
  79.9 6.1 copy-start.24
  86.3 4.5 copy-start
  86.5 6.4 copy-start.14
  96.4 163.2 %all-reduce.10.cloned.1.call-start = ((), (), s32[]{:S(2)}) async-start(), calls=%async_computation.2 | async-start | bytes 1048576 | tf_op jit(solution)/shard_map/psum | solution.py:37
  168.2 2.9 copy-start.27
  168.2 2.8 collective-permute-start
  173.9 179.5 %all-reduce.12.cloned.1.call-start = ((), (), s32[]{:S(2)}) async-start(), calls=%async_computation.3 | async-start | bytes 1048576 | tf_op jit(solution)/shard_map/psum | solution.py:37
  260.8 2.9 copy-start.25
  260.8 2.8 collective-permute-start.1
  263.6 89.7 %copy-start.18 = (bf16[128,2048]{0,1:T(8,128)(2,1)}, bf16[128,2048]{0,1:T(8,128)(2,1)S(1)}, u32[]{:S(2)}) copy-start(bf16[128,2048]{0,1:T(8,128)(2,1)S(1)} %bitcast_select_fusion.1) | copy-start | bytes 1572868
  263.7 93.5 %copy-start.29 = (bf16[1,128,64]{1,2,0:T(8,128)(2,1)S(1)}, bf16[1,128,64]{1,2,0:T(8,128)(2,1)}, u32[]{:S(2)}) copy-start(bf16[1,128,64]{1,2,0:T(8,128)(2,1)} %param.41) | copy-start | bytes 49156
  266.5 234.8 %all-reduce.14.cloned.1.call-start = ((), (), s32[]{:S(2)}) async-start(), calls=%async_computation.4 | async-start | bytes 1048576 | tf_op jit(solution)/shard_map/psum | solution.py:37
  354.6 59.2 %copy-start.26 = (bf16[128,2048]{0,1:T(8,128)(2,1)}, bf16[128,2048]{0,1:T(8,128)(2,1)S(1)}, u32[]{:S(2)}) copy-start(bf16[128,2048]{0,1:T(8,128)(2,1)S(1)} %add_convert_fusion.1) | copy-start | bytes 1572868
  354.6 59.2 %collective-permute-start.2 = (bf16[128,2048]{0,1:T(8,128)(2,1)S(1)}, bf16[128,2048]{0,1:T(8,128)(2,1)}, u32[]{:S(2)}, u32[]{:S(2)}) collective-permute-start(bf16[128,2048]{0,1:T(8,128)(2,1)S(1)} %add_convert_fusion.1), channel_id=1, source_target_pairs={{0,64},{64,128},{128,192},{1,65},{65,129},{129,193},{2,66},{66,130... | collective-permute-start | bytes 1572872 | tf_op jit(solution)/shard_map/ppermute | solution.py:13
  416.3 1.4 copy-start.19
  418.8 174.9 %all-reduce.16.cloned.1.call-start = ((), (), s32[]{:S(2)}) async-start(), calls=%async_computation.5 | async-start | bytes 1048576 | tf_op jit(solution)/shard_map/psum | solution.py:37
  504.4 3.8 collective-permute-start.3
  511.2 180.1 %all-reduce.18.cloned.1.call-start = ((), (), s32[]{:S(2)}) async-start(), calls=%async_computation.7 | async-start | bytes 2097152 | tf_op jit(solution)/shard_map/psum | solution.py:37
  596.6 3.9 collective-permute-start.4
  604.8 206.6 %reduce-scatter.2.cloned.1.call-start = ((), (), s32[]{:S(2)}) async-start(), calls=%async_computation.6 | async-start | bytes 4128768 | tf_op jit(solution)/shard_map/reduce_scatter | solution.py:145
  606.9 4.9 copy-start.10
  606.9 4.9 copy-start.21
  695.0 8.2 %collective-permute-start.5 = (bf16[128,2048]{0,1:T(8,128)(2,1)}, bf16[128,2048]{0,1:T(8,128)(2,1)}, u32[]{:S(2)}, u32[]{:S(2)}) collective-permute-start(bf16[128,2048]{0,1:T(8,128)(2,1)} %fusion.99), channel_id=1, source_target_pairs={{64,0},{128,64},{192,128},{65,1},{129,65},{193,129},{66,2},{130,66... | collective-permute-start | bytes 1572872 | tf_op jit(solution)/shard_map/ppermute | solution.py:13
  698.2 1.0 copy-start.20
  698.5 0.7 copy-start.28
Sparse Core Ops, SparseCore 0:
  96.5 70.4 all-reduce.7
  174.0 85.5 all-reduce.9
  266.6 86.7 all-reduce.11
  418.9 82.2 all-reduce.13
  511.3 82.3 all-reduce.15
  604.9 86.2 all-reduce.17
  725.6 85.7 reduce-scatter.1
where the time goes:
time: 831 us; the launch traced here: 820 us
  waiting for transfers between devices  578 us (70%)
  blocking collectives  117 us (14%)
  local copies, waits for them, and re-layouts  59.3 us (7%)
  other arithmetic  22.6 us (3%)
  matrix products  19.8 us (2%)
  between operations  14 us (2%)
  starting transfers between devices  9.3 us (1%)
    psum x6, waiting for transfers between devices, tensor_total(): lax.psum(partial_value.astype(jnp.bfloat16), 'tensor').astype(jnp.float32)  486 us
    reduce_scatter x1, waiting for transfers between devices, shards(): lax.psum_scatter(accumulated.astype(jnp.bfloat16), 'dp', scatter_dimensio...  85.9 us
    all_gather x1, blocking collectives, shards(): lax.all_gather(x_in, ('section', 'tensor'), axis=2, tiled=True)  61.1 us
    all_gather x1, blocking collectives, shards(): lax.all_gather(cotangent, ('section', 'tensor'), axis=2, tiled=True)  55.8 us
    another operation x20, local copies, waits for them, and re-layouts  19.9 us
    unnamed x21, local copies, waits for them, and re-layouts  19.1 us
  transfers between devices with their start and end apart: 13, of which 11 were waited for; matrix products, arithmetic and copies ran while one was open for 2% of the time, Pallas kernels for 0%

commit v1 on v0

v1 whole, which is shorter than its diff:
```python
import functools

import jax
import jax.numpy as jnp
from jax import lax
from jax.experimental import pallas as pl
from jax.experimental.pallas import tpu as pltpu
from jax.sharding import PartitionSpec as P

EPSILON = 1e-05
F32, BF16 = jnp.float32, jnp.bfloat16
CONTRACT_FIRST = (((0,), (0,)), ((), ()))
STREAMS = 2
PIECE = 64


def dot(left, right):
    return jnp.dot(left, right, preferred_element_type=F32)


def chunked(rows):
    half = rows.shape[1] // 2
    return jnp.concatenate([rows[:, :half], rows[:, half:]], axis=0)


def inv_rms(low, high, features):
    square = jnp.sum(low * low, axis=-1, keepdims=True) + jnp.sum(high * high, axis=-1, keepdims=True)
    return lax.rsqrt(square / features + EPSILON)


def kernel(
    sizes, x_ref, c_ref, gain_ref, gate_hbm, up_hbm, down_hbm, out_ref,
    gate, up, down, down_t, gate_up_t, pieces, landing, hc, hn, qc, normed, product, hidden, slopes,
    gate_factor, up_factor, back_hidden, f_out, f_in, b_out, b_in, f_sum, b_sum, tail_out, tail_mid,
    tail_in, q_rows, q_cols, expanded,
    w_sem, piece_send, piece_recv, fs_send, fs_recv, bs_send, bs_recv, fg_send, fg_recv, bg_send, bg_recv,
    back_send, back_recv, own_send, own_recv, e_send, e_recv, q_send, q_recv, t1_send, t1_recv, t2_send,
    t2_recv, go,
):
    sections, tensors, replicas = sizes
    s, t, r = lax.axis_index("section"), lax.axis_index("tensor"), lax.axis_index("dp")
    last = sections - 1
    features = down.shape[1]
    half = features // 2
    units = gate.shape[1]
    rows = normed.shape[0]
    offsets = sorted(range(1, tensors), key=lambda d: (-min(d, tensors - d), d))
    me = s * tensors + t

    def remote(src, dst, send, recv, **where):
        return pltpu.make_async_remote_copy(
            src_ref=src, dst_ref=dst, send_sem=send, recv_sem=recv, device_id=where,
            device_id_type=pl.DeviceIdType.MESH,
        )

    def other(d):
        return lax.rem(t + d, tensors)

    def replica(d):
        return lax.rem(r + d, replicas)

    loads = [
        pltpu.make_async_copy(src.at[0], dst, w_sem.at[i])
        for i, (src, dst) in enumerate(((gate_hbm, gate), (up_hbm, up), (down_hbm, down)))
    ]
    for load in loads:
        load.start()

    barrier = pltpu.get_barrier_semaphore()
    for d in range(1, sections * tensors):
        to = lax.rem(me + d, sections * tensors)
        pl.semaphore_signal(
            barrier, inc=1, device_id={"section": to // tensors, "tensor": lax.rem(to, tensors)},
            device_id_type=pl.DeviceIdType.MESH,
        )
    for d in range(1, replicas):
        pl.semaphore_signal(
            barrier, inc=1, device_id={"dp": replica(d)}, device_id_type=pl.DeviceIdType.MESH
        )
    for which, ref in enumerate((x_ref, c_ref)):
        for a in range(STREAMS):
            block = ref[0, a * rows:(a + 1) * rows, :].astype(F32)
            pieces[which, a] = jnp.concatenate(
                [block[:rows // 2], block[rows // 2:]], axis=1
            ).astype(BF16)
    pl.semaphore_wait(barrier, sections * tensors + replicas - 2)

    def piece_copy(which, a, d):
        return remote(
            pieces.at[which, a], landing.at[a, me], piece_send.at[which, a, d], piece_recv.at[a, me],
            section=0 if which == 0 else last, tensor=other(d),
        )

    def each_piece(action):
        for which, home in ((0, 0), (1, last)):
            for a in range(STREAMS):
                for d in offsets:
                    action(piece_copy(which, a, d))

                @pl.when(s != home)
                def _():
                    action(piece_copy(which, a, 0))

    each_piece(lambda copy: copy.start())

    def gather_pieces(which, a, dst):
        landing[a, me] = pieces[which, a]

        @pl.loop(1, sections * tensors)
        def _(d):
            src = lax.rem(me + d, sections * tensors)
            remote(
                pieces.at[which, a], landing.at[a, src], piece_send.at[which, a, 0], piece_recv.at[a, src],
                tensor=other(1),
            ).wait_recv()

        left = lax.broadcasted_iota(jnp.int32, (rows // 2, 2 * PIECE), 1) < PIECE

        def block(j):
            first, second = landing[a, 2 * j].astype(F32), landing[a, 2 * j + 1].astype(F32)
            top = jnp.where(left, first, pltpu.roll(second, PIECE, 1))
            bottom = jnp.where(left, pltpu.roll(first, PIECE, 1), second)
            return jnp.concatenate([top, bottom], axis=0)

        for j in range(half // 128):
            low, high = block(j), block(j + half // 128)
            for o in range(tensors):
                part = slice(8 * o, 8 * o + 8)
                dst[a, o, :, 128 * j:128 * j + 128] = jnp.concatenate(
                    [low[part], high[part]], axis=0
                ).astype(BF16)

    def wait_chunks(buffer, send, recv, a):
        for d in reversed(offsets):
            src = other(d)
            remote(buffer.at[a, src], buffer.at[a, src], send.at[a, 0], recv.at[a, src], tensor=other(1)).wait_recv()

    def halves(chunk):
        return chunk[:8], chunk[8:]

    def normalize(buffer, a):
        gain = gain_ref[...]
        for k in range(tensors // 2):
            pair = []
            for o in (2 * k, 2 * k + 1):
                low, high = halves(buffer[a, o].astype(F32))
                scale = inv_rms(low, high, features)
                pair.append(
                    jnp.concatenate([low * scale * gain[:, :half], high * scale * gain[:, half:]], axis=1)
                )
            normed[16 * k:16 * k + 16, :] = jnp.concatenate(pair, axis=0).astype(BF16)

    def fill_q_rows(a):
        for k in range(tensors // 2):
            pair = [
                jnp.concatenate(halves(qc[a, o].astype(F32)), axis=1) for o in (2 * k, 2 * k + 1)
            ]
            q_rows[a, 16 * k:16 * k + 16, :] = jnp.concatenate(pair, axis=0).astype(BF16)

    def scatter(out, land, send, recv, a):
        for o in range(tensors):
            out[a, o] = chunked(product[8 * o:8 * o + 8, :]).astype(BF16)
        for d in offsets:
            remote(out.at[a, other(d)], land.at[a, t], send.at[a, d], recv.at[a, t], tensor=other(d)).start()

    def scatter_sent(out, land, send, recv, a):
        for d in offsets:
            remote(out.at[a, other(d)], land.at[a, t], send.at[a, d], recv.at[a, t], tensor=other(d)).wait_send()

    def summed(out, land, send, recv, a):
        total = out[a, t].astype(F32)
        for d in reversed(offsets):
            src = other(d)
            remote(land.at[a, src], land.at[a, src], send.at[a, 0], recv.at[a, src], tensor=other(1)).wait_recv()
            total = total + land[a, src].astype(F32)
        return total

    def spread(src, dst, send, recv, a, section):
        return [
            remote(src.at[a], dst.at[a, t], send.at[a, d], recv.at[a, t], section=section, tensor=other(d))
            for d in (*offsets, 0)
        ]

    def own_spread(a):
        return [
            remote(f_sum.at[a], hn.at[a, t], own_send.at[a, d], own_recv.at[a, t], tensor=other(d))
            for d in offsets
        ]

    def send_back(a):
        return remote(
            hc.at[a], hn.at[a], back_send.at[a], back_recv.at[a], section=jnp.maximum(s - 1, 0), tensor=t
        )

    def e_copy(d):
        return remote(expanded.at[r], expanded.at[r], e_send.at[d], e_recv.at[r], dp=replica(d))

    def q_copy(d):
        width = q_cols.shape[-1]
        columns = pl.ds(pl.multiple_of(replica(d) * width, width), width)
        return remote(q_rows.at[:, :, columns], q_cols.at[r], q_send.at[d], q_recv.at[r], dp=replica(d))

    def send_q():
        width = q_cols.shape[-1]
        for d in range(1, replicas):
            q_copy(d).start()
        q_cols[r] = q_rows[:, :, pl.ds(pl.multiple_of(r * width, width), width)]

    def tail_copy(a, d):
        return remote(
            tail_out.at[a, replica(d)], tail_mid.at[a, r], t1_send.at[a, d], t1_recv.at[a, r], dp=replica(d)
        )

    def owner_forward(a):
        total = summed(f_out, f_in, fs_send, fs_recv, a)
        f_sum[a] = (hc[a, t].astype(F32) + total).astype(BF16)

    def owner_backward(a):
        grad_low, grad_high = halves(summed(b_out, b_in, bs_send, bs_recv, a))
        low, high = halves(hc[a, t].astype(F32))
        q_low, q_high = halves(qc[a, t].astype(F32))
        gain = gain_ref[...]
        scale = inv_rms(low, high, features)
        w_low, w_high = grad_low * gain[:, :half], grad_high * gain[:, half:]
        mean = (
            jnp.sum(low * w_low, axis=-1, keepdims=True) + jnp.sum(high * w_high, axis=-1, keepdims=True)
        ) / features
        pull = scale * scale * scale * mean
        q_low = q_low + scale * w_low - low * pull
        q_high = q_high + scale * w_high - high * pull
        return q_low, q_high

    def backward_product(a, incoming):
        slopes[:, :units] = (incoming * gate_factor[a]).astype(BF16)
        slopes[:, units:] = (incoming * up_factor[a]).astype(BF16)
        product[...] = dot(slopes[...], gate_up_t[...])
        scatter(b_out, b_in, bs_send, bs_recv, a)

    def pass_back(a):
        q_low, q_high = owner_backward(a)
        b_sum[a] = jnp.concatenate([q_low, q_high], axis=0).astype(BF16)
        for copy in spread(b_sum, qc, bg_send, bg_recv, a, jnp.maximum(s - 1, 0)):
            copy.start()

    def expand(a):
        normalize(hn, a)
        gate_new = dot(normed[...], gate[...])
        up_new = dot(normed[...], up[...])
        expanded[r, a] = (gate_new / (1.0 + jnp.exp(-gate_new)) * up_new).astype(BF16)

    for load in loads:
        load.wait()

    @pl.when(s > 0)
    def _():
        @pl.loop(0, features // 256)
        def _(j):
            part = pl.ds(pl.multiple_of(256 * j, 256), 256)
            down_t[part, :] = down[:, part].T
            gate_up_t[:units, part] = gate[part, :].T
            gate_up_t[units:, part] = up[part, :].T

    @pl.when(s == last)
    def _():
        @pl.loop(0, STREAMS)
        def _(a):
            gather_pieces(1, a, qc)
            fill_q_rows(a)
            back_hidden[a] = dot(q_rows[a], down_t[...])

        send_q()

    @pl.loop(0, STREAMS)
    def _(a):
        @pl.when(s == 0)
        def _():
            gather_pieces(0, a, hc)

        @pl.when(s > 0)
        def _():
            wait_chunks(hc, fg_send, fg_recv, a)
            remote(hc.at[a, t], hc.at[a, t], fg_send.at[a, 0], fg_recv.at[a, t], tensor=other(1)).wait_recv()
            send_back(a).start()

        normalize(hc, a)
        gate_pre = dot(normed[...], gate[...])
        up_pre = dot(normed[...], up[...])
        sigmoid = 1.0 / (1.0 + jnp.exp(-gate_pre))
        silu = gate_pre * sigmoid
        hidden[a] = (silu * up_pre).astype(BF16)
        up_factor[a] = silu
        gate_factor[a] = up_pre * sigmoid * (1.0 + gate_pre * (1.0 - sigmoid))

        @pl.when(s < last)
        def _():
            product[...] = dot(hidden[a], down[...])
            scatter(f_out, f_in, fs_send, fs_recv, a)

        @pl.when(s == last)
        def _():
            backward_product(a, back_hidden[a])

    @pl.when(s < last)
    def _():
        @pl.loop(0, STREAMS)
        def _(a):
            owner_forward(a)
            for copy in spread(f_sum, hc, fg_send, fg_recv, a, jnp.minimum(s + 1, last)):
                copy.start()

        @pl.loop(0, STREAMS)
        def _(a):
            send_back(a).wait_recv()
            expand(a)

        for d in range(1, replicas):
            e_copy(d).start()

    @pl.when(jnp.logical_and(s > 0, s < last))
    def _():
        @pl.loop(0, STREAMS)
        def _(a):
            wait_chunks(qc, bg_send, bg_recv, a)
            remote(qc.at[a, t], qc.at[a, t], bg_send.at[a, 0], bg_recv.at[a, t], tensor=other(1)).wait_recv()
            fill_q_rows(a)
            backward_product(a, dot(q_rows[a], down_t[...]))

    @pl.when(s > 1)
    def _():
        @pl.loop(0, STREAMS)
        def _(a):
            pass_back(a)

    @pl.when(s == last - 1)
    def _():
        pl.semaphore_signal(
            go, inc=1, device_id={"section": last, "tensor": t}, device_id_type=pl.DeviceIdType.MESH
        )

    @pl.when(s == 1)
    def _():
        @pl.loop(0, STREAMS)
        def _(a):
            sides = owner_backward(a)
            width = q_cols.shape[-1]
            for k in range(replicas):
                side = sides[(k * width) // half]
                at = (k * width) % half
                tail_out[a, k] = jnp.concatenate(
                    [side[:, at:at + 128], side[:, at + 128:at + 256]], axis=0
                ).astype(BF16)
            for d in range(1, replicas):
                tail_copy(a, d).start()
            tail_mid[a, r] = tail_out[a, r]

        @pl.loop(0, STREAMS)
        def _(a):
            for d in range(1, replicas):
                src = replica(d)
                remote(
                    tail_mid.at[a, src], tail_mid.at[a, src], t1_send.at[a, 0], t1_recv.at[a, src], dp=replica(1)
                ).wait_recv()
            for copy in spread(tail_mid, tail_in, t2_send, t2_recv, a, 0):
                copy.start()

    @pl.when(jnp.logical_and(s > 0, s < last))
    def _():
        send_q()

    @pl.when(s == last)
    def _():
        pl.semaphore_wait(go, 1)

        @pl.loop(0, STREAMS)
        def _(a):
            product[...] = dot(hidden[a], down[...])
            scatter(f_out, f_in, fs_send, fs_recv, a)

        @pl.loop(0, STREAMS)
        def _(a):
            owner_forward(a)
            hn[a, t] = f_sum[a]
            for copy in own_spread(a):
                copy.start()

        @pl.loop(0, STREAMS)
        def _(a):
            wait_chunks(hn, own_send, own_recv, a)
            expand(a)

        for d in range(1, replicas):
            e_copy(d).start()

    @pl.when(s > 0)
    def _():
        for d in range(1, replicas):
            src = replica(d)
            remote(q_cols.at[src], q_cols.at[src], q_send.at[0], q_recv.at[src], dp=replica(1)).wait_recv()

    for d in range(1, replicas):
        src = replica(d)
        remote(expanded.at[src], expanded.at[src], e_send.at[0], e_recv.at[src], dp=replica(1)).wait_recv()

    @pl.when(s == 0)
    def _():
        @pl.loop(0, STREAMS)
        def _(a):
            wait_chunks(tail_in, t2_send, t2_recv, a)
            remote(tail_in.at[a, t], tail_in.at[a, t], t2_send.at[a, 0], t2_recv.at[a, t], tensor=other(1)).wait_recv()
            for k in range(replicas):
                for pair in range(tensors // 2):
                    both = [
                        jnp.concatenate(halves(tail_in[a, o, k].astype(F32)), axis=1)
                        for o in (2 * pair, 2 * pair + 1)
                    ]
                    q_cols[k, a, 16 * pair:16 * pair + 16, :] = jnp.concatenate(both, axis=0).astype(BF16)

    every = replicas * STREAMS * rows
    out_ref[0] = lax.dot_general(
        expanded[...].reshape(every, units), q_cols[...].reshape(every, q_cols.shape[-1]),
        CONTRACT_FIRST, preferred_element_type=F32,
    )

    each_piece(lambda copy: copy.wait_send())
    for d in range(1, replicas):
        e_copy(d).wait_send()

    @pl.when(s > 0)
    def _():
        for d in range(1, replicas):
            q_copy(d).wait_send()

    @pl.loop(0, STREAMS)
    def _(a):
        scatter_sent(f_out, f_in, fs_send, fs_recv, a)

        @pl.when(s > 0)
        def _():
            send_back(a).wait_send()
            scatter_sent(b_out, b_in, bs_send, bs_recv, a)

        @pl.when(s < last)
        def _():
            for copy in spread(f_sum, hc, fg_send, fg_recv, a, jnp.minimum(s + 1, last)):
                copy.wait_send()

        @pl.when(s == last)
        def _():
            for copy in own_spread(a):
                copy.wait_send()

        @pl.when(s > 1)
        def _():
            for copy in spread(b_sum, qc, bg_send, bg_recv, a, jnp.maximum(s - 1, 0)):
                copy.wait_send()

        @pl.when(s == 1)
        def _():
            for d in range(1, replicas):
                tail_copy(a, d).wait_send()
            for copy in spread(tail_mid, tail_in, t2_send, t2_recv, a, 0):
                copy.wait_send()


def solution(mesh):
    sections, tensors, replicas = (mesh.shape[name] for name in ("section", "tensor", "dp"))

    def shards(x_in, gate_weight, up_weight, down_weight, norm_gain, cotangent):
        features, units = gate_weight.shape[1:]
        rows = 8 * tensors
        width = features // replicas
        half = features // 2
        vmem, dma = pltpu.VMEM, pltpu.SemaphoreType.DMA
        chunks = vmem((STREAMS, tensors, 16, half), BF16)
        chunk = vmem((STREAMS, 16, half), BF16)
        factor = vmem((STREAMS, rows, units), F32)
        pair = [dma((STREAMS, tensors)), dma((STREAMS, tensors))]
        local = pl.BlockSpec(memory_space=pltpu.VMEM)
        anywhere = pl.BlockSpec(memory_space=pl.ANY)
        return pl.pallas_call(
            functools.partial(kernel, (sections, tensors, replicas)),
            out_shape=jax.ShapeDtypeStruct((1, units, width), F32),
            in_specs=[local, local, local, anywhere, anywhere, anywhere],
            out_specs=local,
            scratch_shapes=[
                vmem((features, units), BF16),
                vmem((features, units), BF16),
                vmem((units, features), BF16),
                vmem((features, units), BF16),
                vmem((2 * units, features), BF16),
                vmem((2, STREAMS, rows // 2, 2 * PIECE), BF16),
                vmem((STREAMS, sections * tensors, rows // 2, 2 * PIECE), BF16),
                chunks, chunks, chunks,
                vmem((rows, features), BF16),
                vmem((rows, features), F32),
                vmem((STREAMS, rows, units), BF16),
                vmem((rows, 2 * units), BF16),
                factor, factor, factor,
                chunks, chunks, chunks, chunks,
                chunk, chunk,
                vmem((STREAMS, replicas, 16, width // 2), BF16),
                vmem((STREAMS, replicas, 16, width // 2), BF16),
                vmem((STREAMS, tensors, replicas, 16, width // 2), BF16),
                vmem((STREAMS, rows, features), BF16),
                vmem((replicas, STREAMS, rows, width), BF16),
                vmem((replicas, STREAMS, rows, units), BF16),
                dma((3,)),
                dma((2, STREAMS, tensors)), dma((STREAMS, sections * tensors)),
                *pair, *pair, *pair, *pair,
                dma((STREAMS,)), dma((STREAMS,)),
                *pair,
                dma((replicas,)), dma((replicas,)),
                dma((replicas,)), dma((replicas,)),
                dma((STREAMS, replicas)), dma((STREAMS, replicas)),
                *pair,
                pltpu.SemaphoreType.REGULAR,
            ],
            compiler_params=pltpu.CompilerParams(
                collective_id=0, has_side_effects=True, vmem_limit_bytes=56 * 1024 * 1024
            ),
            name="expanded_step",
        )(x_in, cotangent, norm_gain, gate_weight, up_weight, down_weight)

    placed = (
        P(None, "dp", ("section", "tensor")),
        P("section", None, "tensor"),
        P("section", None, "tensor"),
        P("section", "tensor", None),
        P("section", None),
        P(None, "dp", ("section", "tensor")),
    )
    return jax.shard_map(
        shards, mesh=mesh, in_specs=placed, out_specs=P("section", "tensor", "dp"), check_vma=False
    )
```

time: 831 us -> 134 us (0.16)
  the two profiles are of different devices: /device:TPU:2 before, /device:TPU:25 now
where the time goes in v1:
time: 134 us; the launch traced here: 133 us
  Pallas kernels  128 us (96%)
  local copies, waits for them, and re-layouts  5.01 us (4%)
    pallas_call x1, Pallas kernels, shards(): pl.pallas_call(functools.partial(kernel, (sections, tensors, replicas)),...  128 us
    unnamed x3, local copies, waits for them, and re-layouts  5.01 us

profile of v1, /device:TPU:25, one launch (start us, length us, event | category | flops | bytes accessed | tf_op | source)
XLA Modules:
  0.0 133.4 jit_solution(15813296649792965426)
XLA Ops:
  0.0 1.4 %copy.7.x_ref = bf16[1,128,64]{2,1,0:T(8,128)(2,1)} copy(bf16[1,128,64]{1,2,0:T(8,128)(2,1)} %param.6) | data formatting | bytes 32768 | tf_op args[0]
  1.4 1.4 %copy.8.c_ref = bf16[1,128,64]{2,1,0:T(8,128)(2,1)} copy(bf16[1,128,64]{1,2,0:T(8,128)(2,1)} %param.11) | data formatting | bytes 32768 | tf_op args[5]
  2.9 128.4 %expanded_step.1 = f32[1,896,256]{2,1,0:T(8,128)} custom-call(bf16[1,128,64]{2,1,0:T(8,128)(2,1)} %copy.7.x_ref, bf16[1,128,64]{2,1,0:T(8,128)(2,1)} %copy.8.c_ref, f32[1,2048]{1,0:T(1,128)} %gain_ref.1, bf16[1,2048,896]{2,1,0:T(8,128)(2,1)} %gate_hbm.1, bf16[1,2048,896]{2,1,0:T(8,128)(2,1)} %up_hbm.1, bf16[1,896,2048]{2,1,0:T(8,128)(2,1)} %down_hbm.1), custom_call_target="tpu_custom_call" | custom-call | tf_op jit(solution)/shard_map/expanded_step/pallas_call | solution.py:480
  131.2 2.2 %copy.10 = f32[1,896,256]{2,1,0:T(8,128)} copy(f32[1,896,256]{2,1,0:T(8,128)} %expanded_step.1) | data formatting | bytes 1835008

commit v2 on v1

--- a/solution.py
+++ b/solution.py
@@ -11,7 +11,6 @@
 F32, BF16 = jnp.float32, jnp.bfloat16
 CONTRACT_FIRST = (((0,), (0,)), ((), ()))
 STREAMS = 2
-PIECE = 64
 
 
 def dot(left, right):
@@ -30,7 +29,7 @@
 
 def kernel(
     sizes, x_ref, c_ref, gain_ref, gate_hbm, up_hbm, down_hbm, out_ref,
-    gate, up, down, down_t, gate_up_t, pieces, landing, hc, hn, qc, normed, product, hidden, slopes,
+    gate_up, down, down_t, gate_up_t, landing, hc, hn, qc, normed, product, hidden, slopes,
     gate_factor, up_factor, back_hidden, f_out, f_in, b_out, b_in, f_sum, b_sum, tail_out, tail_mid,
     tail_in, q_rows, q_cols, expanded,
     w_sem, piece_send, piece_recv, fs_send, fs_recv, bs_send, bs_recv, fg_send, fg_recv, bg_send, bg_recv,
@@ -42,7 +41,7 @@
     last = sections - 1
     features = down.shape[1]
     half = features // 2
-    units = gate.shape[1]
+    units = down.shape[0]
     rows = normed.shape[0]
     offsets = sorted(range(1, tensors), key=lambda d: (-min(d, tensors - d), d))
     me = s * tensors + t
@@ -61,7 +60,9 @@
 
     loads = [
         pltpu.make_async_copy(src.at[0], dst, w_sem.at[i])
-        for i, (src, dst) in enumerate(((gate_hbm, gate), (up_hbm, up), (down_hbm, down)))
+        for i, (src, dst) in enumerate(
+            ((gate_hbm, gate_up.at[:, :units]), (up_hbm, gate_up.at[:, units:]), (down_hbm, down))
+        )
     ]
     for load in loads:
         load.start()
@@ -77,58 +78,48 @@
         pl.semaphore_signal(
             barrier, inc=1, device_id={"dp": replica(d)}, device_id_type=pl.DeviceIdType.MESH
         )
-    for which, ref in enumerate((x_ref, c_ref)):
-        for a in range(STREAMS):
-            block = ref[0, a * rows:(a + 1) * rows, :].astype(F32)
-            pieces[which, a] = jnp.concatenate(
-                [block[:rows // 2], block[rows // 2:]], axis=1
-            ).astype(BF16)
     pl.semaphore_wait(barrier, sections * tensors + replicas - 2)
 
-    def piece_copy(which, a, d):
+    inputs = (x_ref, c_ref)
+
+    def piece_copy(which, d):
         return remote(
-            pieces.at[which, a], landing.at[a, me], piece_send.at[which, a, d], piece_recv.at[a, me],
+            inputs[which].at[0], landing.at[me], piece_send.at[which, d], piece_recv.at[me],
             section=0 if which == 0 else last, tensor=other(d),
         )
 
     def each_piece(action):
         for which, home in ((0, 0), (1, last)):
-            for a in range(STREAMS):
-                for d in offsets:
-                    action(piece_copy(which, a, d))
-
-                @pl.when(s != home)
-                def _():
-                    action(piece_copy(which, a, 0))
+            for d in offsets:
+                action(piece_copy(which, d))
+
+            @pl.when(s != home)
+            def _():
+                action(piece_copy(which, 0))
 
     each_piece(lambda copy: copy.start())
 
-    def gather_pieces(which, a, dst):
-        landing[a, me] = pieces[which, a]
+    def gather_pieces(which, dst):
+        landing[me] = inputs[which][0]
 
         @pl.loop(1, sections * tensors)
         def _(d):
             src = lax.rem(me + d, sections * tensors)
             remote(
-                pieces.at[which, a], landing.at[a, src], piece_send.at[which, a, 0], piece_recv.at[a, src],
-                tensor=other(1),
+                inputs[which].at[0], landing.at[src], piece_send.at[which, 0], piece_recv.at[src], tensor=other(1)
             ).wait_recv()
 
-        left = lax.broadcasted_iota(jnp.int32, (rows // 2, 2 * PIECE), 1) < PIECE
-
         def block(j):
-            first, second = landing[a, 2 * j].astype(F32), landing[a, 2 * j + 1].astype(F32)
-            top = jnp.where(left, first, pltpu.roll(second, PIECE, 1))
-            bottom = jnp.where(left, pltpu.roll(first, PIECE, 1), second)
-            return jnp.concatenate([top, bottom], axis=0)
+            return jnp.concatenate([landing[2 * j].astype(F32), landing[2 * j + 1].astype(F32)], axis=0).T
 
         for j in range(half // 128):
             low, high = block(j), block(j + half // 128)
-            for o in range(tensors):
-                part = slice(8 * o, 8 * o + 8)
-                dst[a, o, :, 128 * j:128 * j + 128] = jnp.concatenate(
-                    [low[part], high[part]], axis=0
-                ).astype(BF16)
+            for a in range(STREAMS):
+                for o in range(tensors):
+                    part = slice(a * rows + 8 * o, a * rows + 8 * o + 8)
+                    dst[a, o, :, 128 * j:128 * j + 128] = jnp.concatenate(
+                        [low[part], high[part]], axis=0
+                    ).astype(BF16)
 
     def wait_chunks(buffer, send, recv, a):
         for d in reversed(offsets):
@@ -192,8 +183,40 @@
             hc.at[a], hn.at[a], back_send.at[a], back_recv.at[a], section=jnp.maximum(s - 1, 0), tensor=t
         )
 
-    def e_copy(d):
-        return remote(expanded.at[r], expanded.at[r], e_send.at[d], e_recv.at[r], dp=replica(d))
+    across = replicas // 2
+    partner = lax.rem(r + across, replicas)
+
+    def along(d):
+        return (r // across) * across + lax.rem(r + d, across)
+
+    def e_copies(a):
+        return [
+            remote(expanded.at[r, a], expanded.at[r, a], e_send.at[a, d], e_recv.at[a, r], dp=to)
+            for d, to in enumerate([partner] + [along(d) for d in range(1, across)])
+        ]
+
+    def e_passed(a):
+        return [
+            remote(
+                expanded.at[partner, a], expanded.at[partner, a], e_send.at[a, across + d],
+                e_recv.at[a, partner], dp=along(d),
+            )
+            for d in range(1, across)
+        ]
+
+    def e_wait(a, src):
+        remote(expanded.at[src, a], expanded.at[src, a], e_send.at[a, 0], e_recv.at[a, src], dp=partner).wait_recv()
+
+    def send_expanded(a):
+        for copy in e_copies(a):
+            copy.start()
+
+    def pass_expanded():
+        @pl.loop(0, STREAMS)
+        def _(a):
+            e_wait(a, partner)
+            for copy in e_passed(a):
+                copy.start()
 
     def q_copy(d):
         width = q_cols.shape[-1]
@@ -244,9 +267,14 @@
 
     def expand(a):
         normalize(hn, a)
-        gate_new = dot(normed[...], gate[...])
-        up_new = dot(normed[...], up[...])
+        both = dot(normed[...], gate_up[...])
+        gate_new, up_new = both[:, :units], both[:, units:]
         expanded[r, a] = (gate_new / (1.0 + jnp.exp(-gate_new)) * up_new).astype(BF16)
+
+    def allow(section):
+        pl.semaphore_signal(
+            go, inc=1, device_id={"section": section, "tensor": t}, device_id_type=pl.DeviceIdType.MESH
+        )
 
     for load in loads:
         load.wait()
@@ -257,25 +285,25 @@
         def _(j):
             part = pl.ds(pl.multiple_of(256 * j, 256), 256)
             down_t[part, :] = down[:, part].T
-            gate_up_t[:units, part] = gate[part, :].T
-            gate_up_t[units:, part] = up[part, :].T
+            gate_up_t[:, part] = gate_up[part, :].T
 
     @pl.when(s == last)
     def _():
-        @pl.loop(0, STREAMS)
-        def _(a):
-            gather_pieces(1, a, qc)
+        gather_pieces(1, qc)
+
+        @pl.loop(0, STREAMS)
+        def _(a):
             fill_q_rows(a)
             back_hidden[a] = dot(q_rows[a], down_t[...])
 
         send_q()
 
+    @pl.when(s == 0)
+    def _():
+        gather_pieces(0, hc)
+
     @pl.loop(0, STREAMS)
     def _(a):
-        @pl.when(s == 0)
-        def _():
-            gather_pieces(0, a, hc)
-
         @pl.when(s > 0)
         def _():
             wait_chunks(hc, fg_send, fg_recv, a)
@@ -283,8 +311,8 @@
             send_back(a).start()
 
         normalize(hc, a)
-        gate_pre = dot(normed[...], gate[...])
-        up_pre = dot(normed[...], up[...])
+        both = dot(normed[...], gate_up[...])
+        gate_pre, up_pre = both[:, :units], both[:, units:]
         sigmoid = 1.0 / (1.0 + jnp.exp(-gate_pre))
         silu = gate_pre * sigmoid
         hidden[a] = (silu * up_pre).astype(BF16)
@@ -311,10 +339,28 @@
         @pl.loop(0, STREAMS)
         def _(a):
             send_back(a).wait_recv()
+
+            @pl.when(jnp.logical_and(s == 1, a == STREAMS - 1))
+            def _():
+                allow(0)
+
             expand(a)
 
-        for d in range(1, replicas):
-            e_copy(d).start()
+            @pl.when(s > 0)
+            def _():
+                send_expanded(a)
+
+    @pl.when(s == 0)
+    def _():
+        pl.semaphore_wait(go, 1)
+
+        @pl.loop(0, STREAMS)
+        def _(a):
+            send_expanded(a)
+
+    @pl.when(s < 2)
+    def _():
+        pass_expanded()
 
     @pl.when(jnp.logical_and(s > 0, s < last))
     def _():
@@ -331,11 +377,13 @@
         def _(a):
             pass_back(a)
 
-    @pl.when(s == last - 1)
-    def _():
-        pl.semaphore_signal(
-            go, inc=1, device_id={"section": last, "tensor": t}, device_id_type=pl.DeviceIdType.MESH
-        )
+            @pl.when(jnp.logical_and(s == last - 1, a == 0))
+            def _():
+                allow(last)
+
+    @pl.when(s == 2)
+    def _():
+        pass_expanded()
 
     @pl.when(s == 1)
     def _():
@@ -387,9 +435,9 @@
         def _(a):
             wait_chunks(hn, own_send, own_recv, a)
             expand(a)
-
-        for d in range(1, replicas):
-            e_copy(d).start()
+            send_expanded(a)
+
+        pass_expanded()
 
     @pl.when(s > 0)
     def _():
@@ -397,9 +445,11 @@
             src = replica(d)
             remote(q_cols.at[src], q_cols.at[src], q_send.at[0], q_recv.at[src], dp=replica(1)).wait_recv()
 
-    for d in range(1, replicas):
-        src = replica(d)
-        remote(expanded.at[src], expanded.at[src], e_send.at[0], e_recv.at[src], dp=replica(1)).wait_recv()
+    @pl.loop(0, STREAMS)
+    def _(a):
+        for d in range(1, replicas):
+            if d != across:
+                e_wait(a, replica(d))
 
     @pl.when(s == 0)
     def _():
@@ -422,9 +472,6 @@
     )
 
     each_piece(lambda copy: copy.wait_send())
-    for d in range(1, replicas):
-        e_copy(d).wait_send()
-
     @pl.when(s > 0)
     def _():
         for d in range(1, replicas):
@@ -433,6 +480,8 @@
     @pl.loop(0, STREAMS)
     def _(a):
         scatter_sent(f_out, f_in, fs_send, fs_recv, a)
+        for copy in (*e_copies(a), *e_passed(a)):
+            copy.wait_send()
 
         @pl.when(s > 0)
         def _():
@@ -483,13 +532,11 @@
             in_specs=[local, local, local, anywhere, anywhere, anywhere],
             out_specs=local,
             scratch_shapes=[
-                vmem((features, units), BF16),
-                vmem((features, units), BF16),
+                vmem((features, 2 * units), BF16),
                 vmem((units, features), BF16),
                 vmem((features, units), BF16),
                 vmem((2 * units, features), BF16),
-                vmem((2, STREAMS, rows // 2, 2 * PIECE), BF16),
-                vmem((STREAMS, sections * tensors, rows // 2, 2 * PIECE), BF16),
+                vmem((sections * tensors, *x_in.shape[:0:-1]), BF16),
                 chunks, chunks, chunks,
                 vmem((rows, features), BF16),
                 vmem((rows, features), F32),
@@ -505,11 +552,11 @@
                 vmem((replicas, STREAMS, rows, width), BF16),
                 vmem((replicas, STREAMS, rows, units), BF16),
                 dma((3,)),
-                dma((2, STREAMS, tensors)), dma((STREAMS, sections * tensors)),
+                dma((2, tensors)), dma((sections * tensors,)),
                 *pair, *pair, *pair, *pair,
                 dma((STREAMS,)), dma((STREAMS,)),
                 *pair,
-                dma((replicas,)), dma((replicas,)),
+                dma((STREAMS, replicas)), dma((STREAMS, replicas)),
                 dma((replicas,)), dma((replicas,)),
                 dma((STREAMS, replicas)), dma((STREAMS, replicas)),
                 *pair,
@@ -519,7 +566,7 @@
                 collective_id=0, has_side_effects=True, vmem_limit_bytes=56 * 1024 * 1024
             ),
             name="expanded_step",
-        )(x_in, cotangent, norm_gain, gate_weight, up_weight, down_weight)
+        )(jnp.swapaxes(x_in, 1, 2), jnp.swapaxes(cotangent, 1, 2), norm_gain, gate_weight, up_weight, down_weight)
 
     placed = (
         P(None, "dp", ("section", "tensor")),

time: 134 us -> 122 us (0.910)
  the two profiles are of different devices: /device:TPU:25 before, /device:TPU:2 now
where the time goes in v2:
time: 122 us; the launch traced here: 121 us
  Pallas kernels  119 us (98%)
  local copies, waits for them, and re-layouts  2.16 us (2%)
    pallas_call x1, Pallas kernels, shards(): pl.pallas_call(functools.partial(kernel, (sections, tensors, replicas)),...  119 us

profile of v2, /device:TPU:2, one launch (start us, length us, event | category | flops | bytes accessed | tf_op | source)
XLA Modules:
  0.0 121.2 jit_solution(13144350068270106670)
XLA Ops:
  0.0 119.0 %expanded_step.1 = f32[1,896,256]{2,1,0:T(8,128)} custom-call(bf16[1,64,128]{2,1,0:T(8,128)(2,1)} %bitcast.2, bf16[1,64,128]{2,1,0:T(8,128)(2,1)} %bitcast.3, f32[1,2048]{1,0:T(1,128)} %gain_ref.1, bf16[1,2048,896]{2,1,0:T(8,128)(2,1)} %gate_hbm.1, bf16[1,2048,896]{2,1,0:T(8,128)(2,1)} %up_hbm.1, bf16[1,896,2048]{2,1,0:T(8,128)(2,1)} %down_hbm.1), custom_call_target="tpu_custom_call" | custom-call | tf_op jit(solution)/shard_map/expanded_step/pallas_call | solution.py:529
  119.0 2.2 %copy.8 = f32[1,896,256]{2,1,0:T(8,128)} copy(f32[1,896,256]{2,1,0:T(8,128)} %expanded_step.1) | data formatting | bytes 1835008

commit v3 on v2

v3 whole, which is shorter than its diff:
```python
import functools

import jax
import jax.numpy as jnp
from jax import lax
from jax.experimental import pallas as pl
from jax.experimental.pallas import tpu as pltpu
from jax.sharding import PartitionSpec as P

EPSILON = 1e-05
F32, BF16 = jnp.float32, jnp.bfloat16
CONTRACT_FIRST = (((0,), (0,)), ((), ()))
STREAMS = 2
PARTS = 2


def dot(left, right):
    return jnp.dot(left, right, preferred_element_type=F32)


def chunked(rows):
    half = rows.shape[1] // 2
    return jnp.concatenate([rows[:, :half], rows[:, half:]], axis=0)


def unchunked(chunk):
    chunk = chunk.astype(F32)
    return jnp.concatenate([chunk[:8], chunk[8:]], axis=1)


def row_sum(values):
    return jnp.sum(values, axis=-1, keepdims=True)


def kernel(
    sizes, x_ref, c_ref, gain_ref, gate_hbm, up_hbm, down_hbm, out_ref,
    gate_up, down, down_t, gate_up_t, landing, hc, hn, qc, normed, product, hidden, slopes,
    gate_factor, up_factor, back_hidden, f_out, f_in, b_out, b_in, f_sum, b_sum, tail_out, tail_mid,
    tail_in, q_rows, q_cols, expanded,
    w_sem, piece_send, piece_recv, fs_send, fs_recv, bs_send, bs_recv, fg_send, fg_recv, bg_send, bg_recv,
    back_send, back_recv, own_send, own_recv, relay_send, relay_recv, rest_send, rest_recv, e_send, e_recv,
    q_send, q_recv, t1_send, t1_recv, t2_send, t2_recv, go,
):
    sections, tensors, replicas = sizes
    s, t, r = lax.axis_index("section"), lax.axis_index("tensor"), lax.axis_index("dp")
    last = sections - 1
    features = down.shape[1]
    span = features // PARTS
    units = down.shape[0]
    rows = normed.shape[0]
    offsets = sorted(range(1, tensors), key=lambda d: (-min(d, tensors - d), d))
    me = s * tensors + t

    def remote(src, dst, send, recv, **where):
        return pltpu.make_async_remote_copy(
            src_ref=src, dst_ref=dst, send_sem=send, recv_sem=recv, device_id=where,
            device_id_type=pl.DeviceIdType.MESH,
        )

    def other(d):
        return lax.rem(t + d, tensors)

    def replica(d):
        return lax.rem(r + d, replicas)

    loads = [
        pltpu.make_async_copy(src.at[0], dst, w_sem.at[i])
        for i, (src, dst) in enumerate(
            ((gate_hbm, gate_up.at[:, :units]), (up_hbm, gate_up.at[:, units:]), (down_hbm, down))
        )
    ]
    for load in loads:
        load.start()

    barrier = pltpu.get_barrier_semaphore()
    for d in range(1, sections * tensors):
        to = lax.rem(me + d, sections * tensors)
        pl.semaphore_signal(
            barrier, inc=1, device_id={"section": to // tensors, "tensor": lax.rem(to, tensors)},
            device_id_type=pl.DeviceIdType.MESH,
        )
    for d in range(1, replicas):
        pl.semaphore_signal(
            barrier, inc=1, device_id={"dp": replica(d)}, device_id_type=pl.DeviceIdType.MESH
        )
    pl.semaphore_wait(barrier, sections * tensors + replicas - 2)

    inputs = (x_ref, c_ref)

    def piece_copy(which, d):
        return remote(
            inputs[which].at[0], landing.at[me], piece_send.at[which, d], piece_recv.at[me],
            section=0 if which == 0 else last, tensor=other(d),
        )

    def each_piece(which, action):
        home = 0 if which == 0 else last
        for d in offsets:
            action(piece_copy(which, d))

        @pl.when(s != home)
        def _():
            action(piece_copy(which, 0))

    each_piece(0, lambda copy: copy.start())

    def gather_pieces(which, dst):
        landing[me] = inputs[which][0]

        @pl.loop(1, sections * tensors)
        def _(d):
            src = lax.rem(me + d, sections * tensors)
            remote(
                inputs[which].at[0], landing.at[src], piece_send.at[which, 0], piece_recv.at[src], tensor=other(1)
            ).wait_recv()

        def block(j):
            return jnp.concatenate([landing[2 * j].astype(F32), landing[2 * j + 1].astype(F32)], axis=0).T

        blocks = span // 256
        for p in range(PARTS):
            for j in range(blocks):
                low, high = block(2 * p * blocks + j), block((2 * p + 1) * blocks + j)
                for a in range(STREAMS):
                    for o in range(tensors):
                        part = slice(a * rows + 8 * o, a * rows + 8 * o + 8)
                        dst[a, p, o, :, 128 * j:128 * j + 128] = jnp.concatenate(
                            [low[part], high[part]], axis=0
                        ).astype(BF16)

    def wait_chunk(buffer, send, recv, a, p, src):
        remote(
            buffer.at[a, p, src], buffer.at[a, p, src], send.at[a, p, 0], recv.at[a, p, src], tensor=other(1)
        ).wait_recv()

    def wait_chunks(buffer, send, recv, a, p):
        for d in (0, *reversed(offsets)):
            wait_chunk(buffer, send, recv, a, p, other(d))

    def columns(p):
        return slice(p * span, (p + 1) * span)

    def gated(buffer, a, ready):
        square, both = 0.0, 0.0
        for p in range(PARTS):
            ready(p)
            gain = gain_ref[:, columns(p)]
            squares = []
            for k in range(tensors // 2):
                pair = [unchunked(buffer[a, p, o]) for o in (2 * k, 2 * k + 1)]
                squares += [row_sum(v * v) for v in pair]
                normed[16 * k:16 * k + 16, columns(p)] = (jnp.concatenate(pair, axis=0) * gain).astype(BF16)
            square = square + jnp.concatenate(squares, axis=0)
            both = both + dot(normed[:, columns(p)], gate_up[columns(p), :])
        both = both * lax.rsqrt(square / features + EPSILON)
        return both[:, :units], both[:, units:]

    def fill_q_rows(a, p):
        for k in range(tensors // 2):
            pair = [unchunked(qc[a, p, o]) for o in (2 * k, 2 * k + 1)]
            q_rows[a, 16 * k:16 * k + 16, columns(p)] = jnp.concatenate(pair, axis=0).astype(BF16)

    def back_product(a, ready):
        total = 0.0
        for p in range(PARTS):
            ready(p)
            fill_q_rows(a, p)
            total = total + dot(q_rows[a, :, columns(p)], down_t[columns(p), :])
        return total

    def fill(out, a, p, left, right):
        product[p] = dot(left, right[:, columns(p)])
        for o in range(tensors):
            out[a, p, o] = chunked(product[p, 8 * o:8 * o + 8, :]).astype(BF16)

    def scatter_copies(out, land, send, recv, a, p):
        return [
            remote(
                out.at[a, p, other(d)], land.at[a, p, t], send.at[a, p, d], recv.at[a, p, t], tensor=other(d)
            )
            for d in offsets
        ]

    def scatter(out, land, send, recv, a, p):
        for copy in scatter_copies(out, land, send, recv, a, p):
            copy.start()

    def summed(out, land, send, recv, a, p):
        total = out[a, p, t].astype(F32)
        for d in reversed(offsets):
            wait_chunk(land, send, recv, a, p, other(d))
            total = total + land[a, p, other(d)].astype(F32)
        return total

    def spread_copies(src, dst, send, recv, a, p, section):
        return [
            remote(
                src.at[a, p], dst.at[a, p, t], send.at[a, p, d], recv.at[a, p, t], section=section,
                tensor=other(d),
            )
            for d in (*offsets, 0)
        ]

    def forward_copies(a, p):
        return spread_copies(f_sum, hc, fg_send, fg_recv, a, p, jnp.minimum(s + 1, last))

    def backward_copies(a, p):
        return spread_copies(b_sum, qc, bg_send, bg_recv, a, p, jnp.maximum(s - 1, 0))

    def own_copies(a, p):
        return spread_copies(b_sum, hn, own_send, own_recv, a, p, last)

    def relay_copy(a):
        return remote(f_out.at[a], b_out.at[a], relay_send.at[a], relay_recv.at[a], section=0, tensor=t)

    def rest_copy(a):
        return remote(hc.at[a, :, t], qc.at[a, :, t], rest_send.at[a], rest_recv.at[a], section=0, tensor=t)

    def send_back(a):
        return remote(
            hc.at[a], hn.at[a], back_send.at[a], back_recv.at[a], section=jnp.maximum(s - 1, 0), tensor=t
        )

    across = replicas // 2
    partner = lax.rem(r + across, replicas)

    def along(d):
        return (r // across) * across + lax.rem(r + d, across)

    def e_copies(a):
        return [
            remote(expanded.at[r, a], expanded.at[r, a], e_send.at[a, d], e_recv.at[a, r], dp=to)
            for d, to in enumerate([partner] + [along(d) for d in range(1, across)])
        ]

    def e_passed(a):
        return [
            remote(
                expanded.at[partner, a], expanded.at[partner, a], e_send.at[a, across + d],
                e_recv.at[a, partner], dp=along(d),
            )
            for d in range(1, across)
        ]

    def e_wait(a, src):
        remote(expanded.at[src, a], expanded.at[src, a], e_send.at[a, 0], e_recv.at[a, src], dp=partner).wait_recv()

    def send_expanded(a):
        for copy in e_copies(a):
            copy.start()

    def pass_expanded():
        @pl.loop(0, STREAMS)
        def _(a):
            e_wait(a, partner)
            for copy in e_passed(a):
                copy.start()

    def q_copy(d):
        width = q_cols.shape[-1]
        columns = pl.ds(pl.multiple_of(replica(d) * width, width), width)
        return remote(q_rows.at[:, :, columns], q_cols.at[r], q_send.at[d], q_recv.at[r], dp=replica(d))

    def send_q():
        width = q_cols.shape[-1]
        for d in range(1, replicas):
            q_copy(d).start()
        q_cols[r] = q_rows[:, :, pl.ds(pl.multiple_of(r * width, width), width)]

    def tail_copy(a, d):
        return remote(
            tail_out.at[a, replica(d)], tail_mid.at[a, r], t1_send.at[a, d], t1_recv.at[a, r], dp=replica(d)
        )

    def tail_spread(a):
        return [
            remote(
                tail_mid.at[a], tail_in.at[a, t], t2_send.at[a, d], t2_recv.at[a, t], section=0, tensor=other(d)
            )
            for d in (*offsets, 0)
        ]

    def owner_backward(a):
        grad = jnp.concatenate(
            [unchunked(summed(b_out, b_in, bs_send, bs_recv, a, p)) for p in range(PARTS)], axis=1
        )
        value = jnp.concatenate([unchunked(hc[a, p, t]) for p in range(PARTS)], axis=1)
        before = jnp.concatenate([unchunked(qc[a, p, t]) for p in range(PARTS)], axis=1)
        scale = lax.rsqrt(row_sum(value * value) / features + EPSILON)
        weighted = grad * gain_ref[...]
        pull = scale * scale * scale * (row_sum(value * weighted) / features)
        return before + scale * weighted - value * pull

    def backward_product(a, incoming):
        slopes[:, :units] = (incoming * gate_factor[a]).astype(BF16)
        slopes[:, units:] = (incoming * up_factor[a]).astype(BF16)
        for p in range(PARTS):
            fill(b_out, a, p, slopes[...], gate_up_t)
            scatter(b_out, b_in, bs_send, bs_recv, a, p)

    def pass_back(a):
        row = owner_backward(a)
        for p in range(PARTS):
            b_sum[a, p] = chunked(row[:, columns(p)]).astype(BF16)
            for copy in backward_copies(a, p):
                copy.start()

    def expand(a, ready):
        gate_new, up_new = gated(hn, a, ready)
        expanded[r, a] = (gate_new / (1.0 + jnp.exp(-gate_new)) * up_new).astype(BF16)

    def allow(section):
        pl.semaphore_signal(
            go, inc=1, device_id={"section": section, "tensor": t}, device_id_type=pl.DeviceIdType.MESH
        )

    for load in loads:
        load.wait()

    @pl.when(s > 0)
    def _():
        @pl.loop(0, features // 256)
        def _(j):
            part = pl.ds(pl.multiple_of(256 * j, 256), 256)
            down_t[part, :] = down[:, part].T
            gate_up_t[:, part] = gate_up[part, :].T

    @pl.when(s > 0)
    def _():
        each_piece(1, lambda copy: copy.start())

    @pl.when(s == last)
    def _():
        gather_pieces(1, qc)

        @pl.loop(0, STREAMS)
        def _(a):
            back_hidden[a] = back_product(a, lambda p: None)

        send_q()

    @pl.when(s == 0)
    def _():
        gather_pieces(0, hc)

    @pl.loop(0, STREAMS)
    def _(a):
        def ready(p):
            @pl.when(s > 0)
            def _():
                wait_chunks(hc, fg_send, fg_recv, a, p)

                if p == PARTS - 1:
                    send_back(a).start()

        gate_pre, up_pre = gated(hc, a, ready)
        sigmoid = 1.0 / (1.0 + jnp.exp(-gate_pre))
        silu = gate_pre * sigmoid
        hidden[a] = (silu * up_pre).astype(BF16)
        up_factor[a] = silu
        gate_factor[a] = up_pre * sigmoid * (1.0 + gate_pre * (1.0 - sigmoid))

        @pl.when(s < last)
        def _():
            for p in range(PARTS):
                fill(f_out, a, p, hidden[a], down)
                scatter(f_out, f_in, fs_send, fs_recv, a, p)

        @pl.when(s == last)
        def _():
            backward_product(a, back_hidden[a])

    @pl.when(s == last)
    def _():
        @pl.loop(0, STREAMS)
        def _(a):
            for p in range(PARTS):
                fill(f_out, a, p, hidden[a], down)
            for copy in (relay_copy(a), rest_copy(a)):
                copy.start()

    @pl.when(s < last)
    def _():
        @pl.loop(0, STREAMS)
        def _(a):
            for p in range(PARTS):
                total = summed(f_out, f_in, fs_send, fs_recv, a, p)
                f_sum[a, p] = (hc[a, p, t].astype(F32) + total).astype(BF16)
                for copy in forward_copies(a, p):
                    copy.start()

        @pl.when(s == 0)
        def _():
            each_piece(1, lambda copy: copy.start())

        @pl.loop(0, STREAMS)
        def _(a):
            send_back(a).wait_recv()

            @pl.when(jnp.logical_and(s == 1, a == STREAMS - 1))
            def _():
                allow(0)

            expand(a, lambda p: None)

            @pl.when(s > 0)
            def _():
                send_expanded(a)

    @pl.when(s == 0)
    def _():
        pl.semaphore_wait(go, 1)

        @pl.loop(0, STREAMS)
        def _(a):
            send_expanded(a)

    @pl.when(s < 2)
    def _():
        pass_expanded()

    @pl.when(s == 0)
    def _():
        @pl.loop(0, STREAMS)
        def _(a):
            relay_copy(a).wait_recv()
            for p in range(PARTS):
                scatter(b_out, b_in, bs_send, bs_recv, a, p)

        @pl.loop(0, STREAMS)
        def _(a):
            rest_copy(a).wait_recv()
            for p in range(PARTS):
                total = summed(b_out, b_in, bs_send, bs_recv, a, p)
                b_sum[a, p] = (qc[a, p, t].astype(F32) + total).astype(BF16)
                for copy in own_copies(a, p):
                    copy.start()

    @pl.when(jnp.logical_and(s > 0, s < last))
    def _():
        @pl.loop(0, STREAMS)
        def _(a):
            backward_product(
                a, back_product(a, lambda p: wait_chunks(qc, bg_send, bg_recv, a, p))
            )

        send_q()

    @pl.when(s > 1)
    def _():
        @pl.loop(0, STREAMS)
        def _(a):
            pass_back(a)

    @pl.when(s == 2)
    def _():
        pass_expanded()

    @pl.when(s == 1)
    def _():
        @pl.loop(0, STREAMS)
        def _(a):
            row = owner_backward(a)
            width = q_cols.shape[-1]
            for k in range(replicas):
                tail_out[a, k] = chunked(row[:, k * width:(k + 1) * width]).astype(BF16)
            for d in range(1, replicas):
                tail_copy(a, d).start()
            tail_mid[a, r] = tail_out[a, r]

        @pl.loop(0, STREAMS)
        def _(a):
            for d in range(1, replicas):
                src = replica(d)
                remote(
                    tail_mid.at[a, src], tail_mid.at[a, src], t1_send.at[a, 0], t1_recv.at[a, src], dp=replica(1)
                ).wait_recv()
            for copy in tail_spread(a):
                copy.start()

    @pl.when(s == last)
    def _():
        @pl.loop(0, STREAMS)
        def _(a):
            expand(a, lambda p: wait_chunks(hn, own_send, own_recv, a, p))
            send_expanded(a)

        pass_expanded()

    @pl.when(s > 0)
    def _():
        for d in range(1, replicas):
            src = replica(d)
            remote(q_cols.at[src], q_cols.at[src], q_send.at[0], q_recv.at[src], dp=replica(1)).wait_recv()

    @pl.loop(0, STREAMS)
    def _(a):
        for d in range(1, replicas):
            if d != across:
                e_wait(a, replica(d))

    @pl.when(s == 0)
    def _():
        @pl.loop(0, STREAMS)
        def _(a):
            for d in (0, *reversed(offsets)):
                src = other(d)
                remote(
                    tail_in.at[a, src], tail_in.at[a, src], t2_send.at[a, 0], t2_recv.at[a, src], tensor=other(1)
                ).wait_recv()
            for k in range(replicas):
                for pair in range(tensors // 2):
                    both = [
                        unchunked(tail_in[a, o, k]) for o in (2 * pair, 2 * pair + 1)
                    ]
                    q_cols[k, a, 16 * pair:16 * pair + 16, :] = jnp.concatenate(both, axis=0).astype(BF16)

    every = replicas * STREAMS * rows
    out_ref[0] = lax.dot_general(
        expanded[...].reshape(every, units), q_cols[...].reshape(every, q_cols.shape[-1]),
        CONTRACT_FIRST, preferred_element_type=F32,
    )

    for which in (0, 1):
        each_piece(which, lambda copy: copy.wait_send())

    @pl.when(s > 0)
    def _():
        for d in range(1, replicas):
            q_copy(d).wait_send()

    @pl.loop(0, STREAMS)
    def _(a):
        for copy in (*e_copies(a), *e_passed(a)):
            copy.wait_send()

        for p in range(PARTS):
            for copy in scatter_copies(b_out, b_in, bs_send, bs_recv, a, p):
                copy.wait_send()

            @pl.when(s < last)
            def _():
                for copy in (*scatter_copies(f_out, f_in, fs_send, fs_recv, a, p), *forward_copies(a, p)):
                    copy.wait_send()

            @pl.when(s > 1)
            def _():
                for copy in backward_copies(a, p):
                    copy.wait_send()

            @pl.when(s == 0)
            def _():
                for copy in own_copies(a, p):
                    copy.wait_send()

        @pl.when(s > 0)
        def _():
            send_back(a).wait_send()

        @pl.when(s == last)
        def _():
            for copy in (relay_copy(a), rest_copy(a)):
                copy.wait_send()

        @pl.when(s == 1)
        def _():
            for d in range(1, replicas):
                tail_copy(a, d).wait_send()
            for copy in tail_spread(a):
                copy.wait_send()


def solution(mesh):
    sections, tensors, replicas = (mesh.shape[name] for name in ("section", "tensor", "dp"))

    def shards(x_in, gate_weight, up_weight, down_weight, norm_gain, cotangent):
        features, units = gate_weight.shape[1:]
        rows = 8 * tensors
        width = features // replicas
        span = features // PARTS
        vmem, dma = pltpu.VMEM, pltpu.SemaphoreType.DMA
        chunks = vmem((STREAMS, PARTS, tensors, 16, span // 2), BF16)
        chunk = vmem((STREAMS, PARTS, 16, span // 2), BF16)
        factor = vmem((STREAMS, rows, units), F32)
        pair = [dma((STREAMS, PARTS, tensors))] * 2
        stream = [dma((STREAMS,))] * 2
        flat = [dma((STREAMS, tensors))] * 2
        local = pl.BlockSpec(memory_space=pltpu.VMEM)
        anywhere = pl.BlockSpec(memory_space=pl.ANY)
        return pl.pallas_call(
            functools.partial(kernel, (sections, tensors, replicas)),
            out_shape=jax.ShapeDtypeStruct((1, units, width), F32),
            in_specs=[local, local, local, anywhere, anywhere, anywhere],
            out_specs=local,
            scratch_shapes=[
                vmem((features, 2 * units), BF16),
                vmem((units, features), BF16),
                vmem((features, units), BF16),
                vmem((2 * units, features), BF16),
                vmem((sections * tensors, *x_in.shape[:0:-1]), BF16),
                chunks, chunks, chunks,
                vmem((rows, features), BF16),
                vmem((PARTS, rows, span), F32),
                vmem((STREAMS, rows, units), BF16),
                vmem((rows, 2 * units), BF16),
                factor, factor, factor,
                chunks, chunks, chunks, chunks,
                chunk, chunk,
                vmem((STREAMS, replicas, 16, width // 2), BF16),
                vmem((STREAMS, replicas, 16, width // 2), BF16),
                vmem((STREAMS, tensors, replicas, 16, width // 2), BF16),
                vmem((STREAMS, rows, features), BF16),
                vmem((replicas, STREAMS, rows, width), BF16),
                vmem((replicas, STREAMS, rows, units), BF16),
                dma((3,)),
                dma((2, tensors)), dma((sections * tensors,)),
                *pair, *pair, *pair, *pair,
                *stream,
                *pair,
                *stream, *stream,
                dma((STREAMS, replicas)), dma((STREAMS, replicas)),
                dma((replicas,)), dma((replicas,)),
                dma((STREAMS, replicas)), dma((STREAMS, replicas)),
                *flat,
                pltpu.SemaphoreType.REGULAR,
            ],
            compiler_params=pltpu.CompilerParams(
                collective_id=0, has_side_effects=True, vmem_limit_bytes=56 * 1024 * 1024
            ),
            name="expanded_step",
        )(jnp.swapaxes(x_in, 1, 2), jnp.swapaxes(cotangent, 1, 2), norm_gain, gate_weight, up_weight, down_weight)

    placed = (
        P(None, "dp", ("section", "tensor")),
        P("section", None, "tensor"),
        P("section", None, "tensor"),
        P("section", "tensor", None),
        P("section", None),
        P(None, "dp", ("section", "tensor")),
    )
    return jax.shard_map(
        shards, mesh=mesh, in_specs=placed, out_specs=P("section", "tensor", "dp"), check_vma=False
    )
```

time: 122 us -> 116 us (0.951)
  Pallas kernels: 119 us -> 113 us
    pallas_call x1, Pallas kernels: 119 us -> 113 us  [shards(): pl.pallas_call(functools.partial(kernel, (sections, tensors, replicas)),...]
where the time goes in v3:
time: 116 us; the launch traced here: 115 us
  Pallas kernels  113 us (97%)
  local copies, waits for them, and re-layouts  2.16 us (2%)
    pallas_call x1, Pallas kernels, shards(): pl.pallas_call(functools.partial(kernel, (sections, tensors, replicas)),...  113 us

profile of v3, /device:TPU:2, one launch (start us, length us, event | category | flops | bytes accessed | tf_op | source)
XLA Modules:
  0.0 115.1 jit_solution(3814945844540488009)
XLA Ops:
  0.0 112.9 %expanded_step.1 = f32[1,896,256]{2,1,0:T(8,128)} custom-call(bf16[1,64,128]{2,1,0:T(8,128)(2,1)} %bitcast.2, bf16[1,64,128]{2,1,0:T(8,128)(2,1)} %bitcast.3, f32[1,2048]{1,0:T(1,128)} %gain_ref.1, bf16[1,2048,896]{2,1,0:T(8,128)(2,1)} %gate_hbm.1, bf16[1,2048,896]{2,1,0:T(8,128)(2,1)} %up_hbm.1, bf16[1,896,2048]{2,1,0:T(8,128)(2,1)} %down_hbm.1), custom_call_target="tpu_custom_call" | custom-call | tf_op jit(solution)/shard_map/expanded_step/pallas_call | solution.py:590
  113.0 2.2 %copy.8 = f32[1,896,256]{2,1,0:T(8,128)} copy(f32[1,896,256]{2,1,0:T(8,128)} %expanded_step.1) | data formatting | bytes 1835008

commit v4 on v3

--- a/solution.py
+++ b/solution.py
@@ -33,8 +33,8 @@
 
 
 def kernel(
-    sizes, x_ref, c_ref, gain_ref, gate_hbm, up_hbm, down_hbm, out_ref,
-    gate_up, down, down_t, gate_up_t, landing, hc, hn, qc, normed, product, hidden, slopes,
+    sizes, x_ref, c_ref, gain_hbm, gate_hbm, up_hbm, down_hbm, out_ref,
+    gain_ref, gate_up, down, down_t, gate_up_t, landing, hc, hn, qc, normed, product, hidden, slopes,
     gate_factor, up_factor, back_hidden, f_out, f_in, b_out, b_in, f_sum, b_sum, tail_out, tail_mid,
     tail_in, q_rows, q_cols, expanded,
     w_sem, piece_send, piece_recv, fs_send, fs_recv, bs_send, bs_recv, fg_send, fg_recv, bg_send, bg_recv,
@@ -64,25 +64,28 @@
         return lax.rem(r + d, replicas)
 
     loads = [
-        pltpu.make_async_copy(src.at[0], dst, w_sem.at[i])
-        for i, (src, dst) in enumerate(
-            ((gate_hbm, gate_up.at[:, :units]), (up_hbm, gate_up.at[:, units:]), (down_hbm, down))
-        )
+        pltpu.make_async_copy(src, dst, w_sem.at[i])
+        for i, (src, dst) in enumerate((
+            (gain_hbm, gain_ref), (gate_hbm.at[0], gate_up.at[:, :units]), (up_hbm.at[0], gate_up.at[:, units:]),
+            (down_hbm.at[0], down),
+        ))
     ]
     for load in loads:
         load.start()
 
     barrier = pltpu.get_barrier_semaphore()
-    for d in range(1, sections * tensors):
-        to = lax.rem(me + d, sections * tensors)
-        pl.semaphore_signal(
-            barrier, inc=1, device_id={"section": to // tensors, "tensor": lax.rem(to, tensors)},
-            device_id_type=pl.DeviceIdType.MESH,
-        )
-    for d in range(1, replicas):
-        pl.semaphore_signal(
-            barrier, inc=1, device_id={"dp": replica(d)}, device_id_type=pl.DeviceIdType.MESH
-        )
+    for d in (*offsets, 0):
+        for k in range(sections):
+            if d or k:
+                pl.semaphore_signal(
+                    barrier, inc=1, device_id={"section": lax.rem(s + k, sections), "tensor": other(d)},
+                    device_id_type=pl.DeviceIdType.MESH,
+                )
+        if d == offsets[0]:
+            for k in range(1, replicas):
+                pl.semaphore_signal(
+                    barrier, inc=1, device_id={"dp": replica(k)}, device_id_type=pl.DeviceIdType.MESH
+                )
     pl.semaphore_wait(barrier, sections * tensors + replicas - 2)
 
     inputs = (x_ref, c_ref)
@@ -104,29 +107,45 @@
 
     each_piece(0, lambda copy: copy.start())
 
-    def gather_pieces(which, dst):
-        landing[me] = inputs[which][0]
-
-        @pl.loop(1, sections * tensors)
-        def _(d):
-            src = lax.rem(me + d, sections * tensors)
-            remote(
-                inputs[which].at[0], landing.at[src], piece_send.at[which, 0], piece_recv.at[src], tensor=other(1)
-            ).wait_recv()
+    def own_piece(which):
+        return pltpu.make_async_copy(inputs[which].at[0], landing.at[me], piece_recv.at[me])
+
+    @pl.when(s == 0)
+    def _():
+        own_piece(0).start()
+
+    @pl.when(s == last)
+    def _():
+        own_piece(1).start()
+
+    def gather_pieces(which, dst, p):
+        count = sections * tensors // PARTS
+
+        @pl.loop(p * count, (p + 1) * count)
+        def _(src):
+            @pl.when(src == me)
+            def _():
+                own_piece(which).wait()
+
+            @pl.when(src != me)
+            def _():
+                remote(
+                    inputs[which].at[0], landing.at[src], piece_send.at[which, 0], piece_recv.at[src],
+                    tensor=other(1),
+                ).wait_recv()
 
         def block(j):
             return jnp.concatenate([landing[2 * j].astype(F32), landing[2 * j + 1].astype(F32)], axis=0).T
 
         blocks = span // 256
-        for p in range(PARTS):
-            for j in range(blocks):
-                low, high = block(2 * p * blocks + j), block((2 * p + 1) * blocks + j)
-                for a in range(STREAMS):
-                    for o in range(tensors):
-                        part = slice(a * rows + 8 * o, a * rows + 8 * o + 8)
-                        dst[a, p, o, :, 128 * j:128 * j + 128] = jnp.concatenate(
-                            [low[part], high[part]], axis=0
-                        ).astype(BF16)
+        for j in range(blocks):
+            low, high = block(2 * p * blocks + j), block((2 * p + 1) * blocks + j)
+            for a in range(STREAMS):
+                for o in range(tensors):
+                    part = slice(a * rows + 8 * o, a * rows + 8 * o + 8)
+                    dst[a, p, o, :, 128 * j:128 * j + 128] = jnp.concatenate(
+                        [low[part], high[part]], axis=0
+                    ).astype(BF16)
 
     def wait_chunk(buffer, send, recv, a, p, src):
         remote(
@@ -309,6 +328,31 @@
         gate_new, up_new = gated(hn, a, ready)
         expanded[r, a] = (gate_new / (1.0 + jnp.exp(-gate_new)) * up_new).astype(BF16)
 
+    def forward_sent():
+        for which in (0, 1):
+            each_piece(which, lambda copy: copy.wait_send())
+
+        @pl.loop(0, STREAMS)
+        def _(a):
+            for copy in e_copies(a):
+                copy.wait_send()
+
+            @pl.when(s > 0)
+            def _():
+                send_back(a).wait_send()
+
+            @pl.when(s < last)
+            def _():
+                for p in range(PARTS):
+                    for copy in (*scatter_copies(f_out, f_in, fs_send, fs_recv, a, p), *forward_copies(a, p)):
+                        copy.wait_send()
+
+    def passed_sent():
+        @pl.loop(0, STREAMS)
+        def _(a):
+            for copy in e_passed(a):
+                copy.wait_send()
+
     def allow(section):
         pl.semaphore_signal(
             go, inc=1, device_id={"section": section, "tensor": t}, device_id_type=pl.DeviceIdType.MESH
@@ -331,21 +375,22 @@
 
     @pl.when(s == last)
     def _():
-        gather_pieces(1, qc)
+        for p in range(PARTS):
+            gather_pieces(1, qc, p)
 
         @pl.loop(0, STREAMS)
         def _(a):
             back_hidden[a] = back_product(a, lambda p: None)
 
         send_q()
-
-    @pl.when(s == 0)
-    def _():
-        gather_pieces(0, hc)
 
     @pl.loop(0, STREAMS)
     def _(a):
         def ready(p):
+            @pl.when(jnp.logical_and(s == 0, a == 0))
+            def _():
+                gather_pieces(0, hc, p)
+
             @pl.when(s > 0)
             def _():
                 wait_chunks(hc, fg_send, fg_recv, a, p)
@@ -418,6 +463,11 @@
     @pl.when(s < 2)
     def _():
         pass_expanded()
+        passed_sent()
+
+    @pl.when(s < last)
+    def _():
+        forward_sent()
 
     @pl.when(s == 0)
     def _():
@@ -435,6 +485,12 @@
                 b_sum[a, p] = (qc[a, p, t].astype(F32) + total).astype(BF16)
                 for copy in own_copies(a, p):
                     copy.start()
+
+        @pl.loop(0, STREAMS)
+        def _(a):
+            for p in range(PARTS):
+                for copy in (*scatter_copies(b_out, b_in, bs_send, bs_recv, a, p), *own_copies(a, p)):
+                    copy.wait_send()
 
     @pl.when(jnp.logical_and(s > 0, s < last))
     def _():
@@ -521,53 +577,41 @@
         CONTRACT_FIRST, preferred_element_type=F32,
     )
 
-    for which in (0, 1):
-        each_piece(which, lambda copy: copy.wait_send())
+    @pl.when(s == last)
+    def _():
+        forward_sent()
+
+    @pl.when(s > 1)
+    def _():
+        passed_sent()
 
     @pl.when(s > 0)
     def _():
         for d in range(1, replicas):
             q_copy(d).wait_send()
 
-    @pl.loop(0, STREAMS)
-    def _(a):
-        for copy in (*e_copies(a), *e_passed(a)):
-            copy.wait_send()
-
-        for p in range(PARTS):
-            for copy in scatter_copies(b_out, b_in, bs_send, bs_recv, a, p):
-                copy.wait_send()
-
-            @pl.when(s < last)
-            def _():
-                for copy in (*scatter_copies(f_out, f_in, fs_send, fs_recv, a, p), *forward_copies(a, p)):
+        @pl.loop(0, STREAMS)
+        def _(a):
+            for p in range(PARTS):
+                for copy in scatter_copies(b_out, b_in, bs_send, bs_recv, a, p):
                     copy.wait_send()
 
-            @pl.when(s > 1)
-            def _():
-                for copy in backward_copies(a, p):
+                @pl.when(s > 1)
+                def _():
+                    for copy in backward_copies(a, p):
+                        copy.wait_send()
+
+            @pl.when(s == last)
+            def _():
+                for copy in (relay_copy(a), rest_copy(a)):
                     copy.wait_send()
 
-            @pl.when(s == 0)
-            def _():
-                for copy in own_copies(a, p):
+            @pl.when(s == 1)
+            def _():
+                for d in range(1, replicas):
+                    tail_copy(a, d).wait_send()
+                for copy in tail_spread(a):
                     copy.wait_send()
-
-        @pl.when(s > 0)
-        def _():
-            send_back(a).wait_send()
-
-        @pl.when(s == last)
-        def _():
-            for copy in (relay_copy(a), rest_copy(a)):
-                copy.wait_send()
-
-        @pl.when(s == 1)
-        def _():
-            for d in range(1, replicas):
-                tail_copy(a, d).wait_send()
-            for copy in tail_spread(a):
-                copy.wait_send()
 
 
 def solution(mesh):
@@ -589,10 +633,11 @@
         anywhere = pl.BlockSpec(memory_space=pl.ANY)
         return pl.pallas_call(
             functools.partial(kernel, (sections, tensors, replicas)),
-            out_shape=jax.ShapeDtypeStruct((1, units, width), F32),
-            in_specs=[local, local, local, anywhere, anywhere, anywhere],
+            out_shape=vmem((1, units, width), F32),
+            in_specs=[anywhere] * 6,
             out_specs=local,
             scratch_shapes=[
+                vmem((1, features), F32),
                 vmem((features, 2 * units), BF16),
                 vmem((units, features), BF16),
                 vmem((features, units), BF16),
@@ -612,7 +657,7 @@
                 vmem((STREAMS, rows, features), BF16),
                 vmem((replicas, STREAMS, rows, width), BF16),
                 vmem((replicas, STREAMS, rows, units), BF16),
-                dma((3,)),
+                dma((4,)),
                 dma((2, tensors)), dma((sections * tensors,)),
                 *pair, *pair, *pair, *pair,
                 *stream,

time: 116 us -> 112 us (0.966)
  Pallas kernels: 113 us -> 111 us
  local copies, waits for them, and re-layouts: 2.16 us -> 0.93 us
    pallas_call x1, Pallas kernels: 113 us -> 111 us  [shards(): pl.pallas_call(functools.partial(kernel, (sections, tensors, replicas)),...]
    unnamed x1, local copies, waits for them, and re-layouts: 2.16 us -> 0.93 us
where the time goes in v4:
time: 112 us
  Pallas kernels  111 us (99%)
    pallas_call x1, Pallas kernels, shards(): pl.pallas_call(functools.partial(kernel, (sections, tensors, replicas)),...  111 us

profile of v4, /device:TPU:2, one launch (start us, length us, event | category | flops | bytes accessed | tf_op | source)
XLA Modules:
  0.0 111.7 jit_solution(14380374027578261040)
XLA Ops:
  0.0 110.8 %expanded_step.1 = f32[1,896,256]{2,1,0:T(8,128)S(1)} custom-call(bf16[1,64,128]{2,1,0:T(8,128)(2,1)} %bitcast.2, bf16[1,64,128]{2,1,0:T(8,128)(2,1)} %bitcast.3, f32[1,2048]{1,0:T(1,128)} %gain_hbm.1, bf16[1,2048,896]{2,1,0:T(8,128)(2,1)} %gate_hbm.1, bf16[1,2048,896]{2,1,0:T(8,128)(2,1)} %up_hbm.1, bf16[1,896,2048]{2,1,0:T(8,128)(2,1)} %down_hbm.1), custom_call_target="tpu_custom_call" | custom-call | tf_op jit(solution)/shard_map/expanded_step/pallas_call | solution.py:634
  110.8 0.9 copy.8

commit v5 on v4

--- a/solution.py
+++ b/solution.py
@@ -34,7 +34,7 @@
 
 def kernel(
     sizes, x_ref, c_ref, gain_hbm, gate_hbm, up_hbm, down_hbm, out_ref,
-    gain_ref, gate_up, down, down_t, gate_up_t, landing, hc, hn, qc, normed, product, hidden, slopes,
+    gain_ref, both, back, square, gate_up, down, down_t, gate_up_t, landing, hc, hn, qc, normed, product, hidden, slopes,
     gate_factor, up_factor, back_hidden, f_out, f_in, b_out, b_in, f_sum, b_sum, tail_out, tail_mid,
     tail_in, q_rows, q_cols, expanded,
     w_sem, piece_send, piece_recv, fs_send, fs_recv, bs_send, bs_recv, fg_send, fg_recv, bg_send, bg_recv,
@@ -157,11 +157,14 @@
             wait_chunk(buffer, send, recv, a, p, other(d))
 
     def columns(p):
-        return slice(p * span, (p + 1) * span)
+        return pl.ds(pl.multiple_of(p * span, span), span)
 
     def gated(buffer, a, ready):
-        square, both = 0.0, 0.0
-        for p in range(PARTS):
+        both[...] = jnp.zeros_like(both)
+        square[...] = jnp.zeros_like(square)
+
+        @pl.loop(0, PARTS)
+        def _(p):
             ready(p)
             gain = gain_ref[:, columns(p)]
             squares = []
@@ -169,10 +172,11 @@
                 pair = [unchunked(buffer[a, p, o]) for o in (2 * k, 2 * k + 1)]
                 squares += [row_sum(v * v) for v in pair]
                 normed[16 * k:16 * k + 16, columns(p)] = (jnp.concatenate(pair, axis=0) * gain).astype(BF16)
-            square = square + jnp.concatenate(squares, axis=0)
-            both = both + dot(normed[:, columns(p)], gate_up[columns(p), :])
-        both = both * lax.rsqrt(square / features + EPSILON)
-        return both[:, :units], both[:, units:]
+            square[...] += jnp.broadcast_to(jnp.concatenate(squares, axis=0), square.shape)
+            both[...] += dot(normed[:, columns(p)], gate_up[columns(p), :])
+
+        product = both[...] * lax.rsqrt(square[:, :1] / features + EPSILON)
+        return product[:, :units], product[:, units:]
 
     def fill_q_rows(a, p):
         for k in range(tensors // 2):
@@ -180,17 +184,20 @@
             q_rows[a, 16 * k:16 * k + 16, columns(p)] = jnp.concatenate(pair, axis=0).astype(BF16)
 
     def back_product(a, ready):
-        total = 0.0
-        for p in range(PARTS):
+        back[...] = jnp.zeros_like(back)
+
+        @pl.loop(0, PARTS)
+        def _(p):
             ready(p)
             fill_q_rows(a, p)
-            total = total + dot(q_rows[a, :, columns(p)], down_t[columns(p), :])
-        return total
+            back[...] += dot(q_rows[a, :, columns(p)], down_t[columns(p), :])
+
+        return back[...]
 
     def fill(out, a, p, left, right):
-        product[p] = dot(left, right[:, columns(p)])
+        product[...] = dot(left, right[:, columns(p)])
         for o in range(tensors):
-            out[a, p, o] = chunked(product[p, 8 * o:8 * o + 8, :]).astype(BF16)
+            out[a, p, o] = chunked(product[8 * o:8 * o + 8, :]).astype(BF16)
 
     def scatter_copies(out, land, send, recv, a, p):
         return [
@@ -313,14 +320,15 @@
     def backward_product(a, incoming):
         slopes[:, :units] = (incoming * gate_factor[a]).astype(BF16)
         slopes[:, units:] = (incoming * up_factor[a]).astype(BF16)
-        for p in range(PARTS):
+        @pl.loop(0, PARTS)
+        def _(p):
             fill(b_out, a, p, slopes[...], gate_up_t)
             scatter(b_out, b_in, bs_send, bs_recv, a, p)
 
     def pass_back(a):
         row = owner_backward(a)
         for p in range(PARTS):
-            b_sum[a, p] = chunked(row[:, columns(p)]).astype(BF16)
+            b_sum[a, p] = chunked(row[:, p * span:(p + 1) * span]).astype(BF16)
             for copy in backward_copies(a, p):
                 copy.start()
 
@@ -395,7 +403,8 @@
             def _():
                 wait_chunks(hc, fg_send, fg_recv, a, p)
 
-                if p == PARTS - 1:
+                @pl.when(p == PARTS - 1)
+                def _():
                     send_back(a).start()
 
         gate_pre, up_pre = gated(hc, a, ready)
@@ -407,7 +416,8 @@
 
         @pl.when(s < last)
         def _():
-            for p in range(PARTS):
+            @pl.loop(0, PARTS)
+            def _(p):
                 fill(f_out, a, p, hidden[a], down)
                 scatter(f_out, f_in, fs_send, fs_recv, a, p)
 
@@ -419,8 +429,10 @@
     def _():
         @pl.loop(0, STREAMS)
         def _(a):
-            for p in range(PARTS):
+            @pl.loop(0, PARTS)
+            def _(p):
                 fill(f_out, a, p, hidden[a], down)
+
             for copy in (relay_copy(a), rest_copy(a)):
                 copy.start()
 
@@ -428,7 +440,8 @@
     def _():
         @pl.loop(0, STREAMS)
         def _(a):
-            for p in range(PARTS):
+            @pl.loop(0, PARTS)
+            def _(p):
                 total = summed(f_out, f_in, fs_send, fs_recv, a, p)
                 f_sum[a, p] = (hc[a, p, t].astype(F32) + total).astype(BF16)
                 for copy in forward_copies(a, p):
@@ -480,7 +493,8 @@
         @pl.loop(0, STREAMS)
         def _(a):
             rest_copy(a).wait_recv()
-            for p in range(PARTS):
+            @pl.loop(0, PARTS)
+            def _(p):
                 total = summed(b_out, b_in, bs_send, bs_recv, a, p)
                 b_sum[a, p] = (qc[a, p, t].astype(F32) + total).astype(BF16)
                 for copy in own_copies(a, p):
@@ -555,27 +569,30 @@
             if d != across:
                 e_wait(a, replica(d))
 
-    @pl.when(s == 0)
-    def _():
-        @pl.loop(0, STREAMS)
-        def _(a):
-            for d in (0, *reversed(offsets)):
-                src = other(d)
-                remote(
-                    tail_in.at[a, src], tail_in.at[a, src], t2_send.at[a, 0], t2_recv.at[a, src], tensor=other(1)
-                ).wait_recv()
-            for k in range(replicas):
-                for pair in range(tensors // 2):
-                    both = [
-                        unchunked(tail_in[a, o, k]) for o in (2 * pair, 2 * pair + 1)
-                    ]
-                    q_cols[k, a, 16 * pair:16 * pair + 16, :] = jnp.concatenate(both, axis=0).astype(BF16)
-
-    every = replicas * STREAMS * rows
-    out_ref[0] = lax.dot_general(
-        expanded[...].reshape(every, units), q_cols[...].reshape(every, q_cols.shape[-1]),
-        CONTRACT_FIRST, preferred_element_type=F32,
-    )
+    def gather_tail(a):
+        for d in (0, *reversed(offsets)):
+            src = other(d)
+            remote(
+                tail_in.at[a, src], tail_in.at[a, src], t2_send.at[a, 0], t2_recv.at[a, src], tensor=other(1)
+            ).wait_recv()
+        for k in range(replicas):
+            for o in range(0, tensors, 2):
+                group = [unchunked(tail_in[a, o + j, k]) for j in range(2)]
+                q_cols[k, a, 8 * o:8 * o + 16, :] = jnp.concatenate(group, axis=0).astype(BF16)
+
+    out_ref[...] = jnp.zeros_like(out_ref)
+
+    @pl.loop(0, STREAMS)
+    def _(a):
+        @pl.when(s == 0)
+        def _():
+            gather_tail(a)
+
+        every = replicas * rows
+        out_ref[0] += lax.dot_general(
+            expanded[:, a].reshape(every, units), q_cols[:, a].reshape(every, q_cols.shape[-1]),
+            CONTRACT_FIRST, preferred_element_type=F32,
+        )
 
     @pl.when(s == last)
     def _():
@@ -638,6 +655,9 @@
             out_specs=local,
             scratch_shapes=[
                 vmem((1, features), F32),
+                vmem((rows, 2 * units), F32),
+                vmem((rows, units), F32),
+                vmem((rows, 128), F32),
                 vmem((features, 2 * units), BF16),
                 vmem((units, features), BF16),
                 vmem((features, units), BF16),
@@ -645,7 +665,7 @@
                 vmem((sections * tensors, *x_in.shape[:0:-1]), BF16),
                 chunks, chunks, chunks,
                 vmem((rows, features), BF16),
-                vmem((PARTS, rows, span), F32),
+                vmem((rows, span), F32),
                 vmem((STREAMS, rows, units), BF16),
                 vmem((rows, 2 * units), BF16),
                 factor, factor, factor,

time: 112 us -> 111 us (level)
  no operation moved by 1% of the time
where the time goes in v5:
time: 111 us
  Pallas kernels  110 us (99%)
    pallas_call x1, Pallas kernels, shards(): pl.pallas_call(functools.partial(kernel, (sections, tensors, replicas)),...  110 us

profile of v5, /device:TPU:2, one launch (start us, length us, event | category | flops | bytes accessed | tf_op | source)
XLA Modules:
  0.0 110.7 jit_solution(6895994248373482903)
XLA Ops:
  0.0 109.8 %expanded_step.1 = f32[1,896,256]{2,1,0:T(8,128)S(1)} custom-call(bf16[1,64,128]{2,1,0:T(8,128)(2,1)} %bitcast.2, bf16[1,64,128]{2,1,0:T(8,128)(2,1)} %bitcast.3, f32[1,2048]{1,0:T(1,128)} %gain_hbm.1, bf16[1,2048,896]{2,1,0:T(8,128)(2,1)} %gate_hbm.1, bf16[1,2048,896]{2,1,0:T(8,128)(2,1)} %up_hbm.1, bf16[1,896,2048]{2,1,0:T(8,128)(2,1)} %down_hbm.1), custom_call_target="tpu_custom_call" | custom-call | tf_op jit(solution)/shard_map/expanded_step/pallas_call | solution.py:651
  109.8 0.9 copy.8

commit v6 on v5

--- a/solution.py
+++ b/solution.py
@@ -282,16 +282,16 @@
             for copy in e_passed(a):
                 copy.start()
 
-    def q_copy(d):
+    def q_copy(a, d):
         width = q_cols.shape[-1]
-        columns = pl.ds(pl.multiple_of(replica(d) * width, width), width)
-        return remote(q_rows.at[:, :, columns], q_cols.at[r], q_send.at[d], q_recv.at[r], dp=replica(d))
-
-    def send_q():
+        part = pl.ds(pl.multiple_of(replica(d) * width, width), width)
+        return remote(q_rows.at[a, :, part], q_cols.at[r, a], q_send.at[a, d], q_recv.at[a, r], dp=replica(d))
+
+    def send_q(a):
         width = q_cols.shape[-1]
         for d in range(1, replicas):
-            q_copy(d).start()
-        q_cols[r] = q_rows[:, :, pl.ds(pl.multiple_of(r * width, width), width)]
+            q_copy(a, d).start()
+        q_cols[r, a] = q_rows[a, :, pl.ds(pl.multiple_of(r * width, width), width)]
 
     def tail_copy(a, d):
         return remote(
@@ -389,8 +389,7 @@
         @pl.loop(0, STREAMS)
         def _(a):
             back_hidden[a] = back_product(a, lambda p: None)
-
-        send_q()
+            send_q(a)
 
     @pl.loop(0, STREAMS)
     def _(a):
@@ -510,11 +509,9 @@
     def _():
         @pl.loop(0, STREAMS)
         def _(a):
-            backward_product(
-                a, back_product(a, lambda p: wait_chunks(qc, bg_send, bg_recv, a, p))
-            )
-
-        send_q()
+            incoming = back_product(a, lambda p: wait_chunks(qc, bg_send, bg_recv, a, p))
+            send_q(a)
+            backward_product(a, incoming)
 
     @pl.when(s > 1)
     def _():
@@ -559,9 +556,13 @@
 
     @pl.when(s > 0)
     def _():
-        for d in range(1, replicas):
-            src = replica(d)
-            remote(q_cols.at[src], q_cols.at[src], q_send.at[0], q_recv.at[src], dp=replica(1)).wait_recv()
+        @pl.loop(0, STREAMS)
+        def _(a):
+            for d in range(1, replicas):
+                src = replica(d)
+                remote(
+                    q_cols.at[src, a], q_cols.at[src, a], q_send.at[a, 0], q_recv.at[a, src], dp=replica(1)
+                ).wait_recv()
 
     @pl.loop(0, STREAMS)
     def _(a):
@@ -604,11 +605,11 @@
 
     @pl.when(s > 0)
     def _():
-        for d in range(1, replicas):
-            q_copy(d).wait_send()
-
-        @pl.loop(0, STREAMS)
-        def _(a):
+        @pl.loop(0, STREAMS)
+        def _(a):
+            for d in range(1, replicas):
+                q_copy(a, d).wait_send()
+
             for p in range(PARTS):
                 for copy in scatter_copies(b_out, b_in, bs_send, bs_recv, a, p):
                     copy.wait_send()
@@ -684,7 +685,7 @@
                 *pair,
                 *stream, *stream,
                 dma((STREAMS, replicas)), dma((STREAMS, replicas)),
-                dma((replicas,)), dma((replicas,)),
+                dma((STREAMS, replicas)), dma((STREAMS, replicas)),
                 dma((STREAMS, replicas)), dma((STREAMS, replicas)),
                 *flat,
                 pltpu.SemaphoreType.REGULAR,

time: 111 us -> 110 us (level)
  no operation moved by 1% of the time
where the time goes in v6:
time: 110 us
  Pallas kernels  109 us (99%)
    pallas_call x1, Pallas kernels, shards(): pl.pallas_call(functools.partial(kernel, (sections, tensors, replicas)),...  109 us

profile of v6, /device:TPU:2, one launch (start us, length us, event | category | flops | bytes accessed | tf_op | source)
XLA Modules:
  0.0 110.4 jit_solution(817794951947421649)
XLA Ops:
  0.0 109.4 %expanded_step.1 = f32[1,896,256]{2,1,0:T(8,128)S(1)} custom-call(bf16[1,64,128]{2,1,0:T(8,128)(2,1)} %bitcast.2, bf16[1,64,128]{2,1,0:T(8,128)(2,1)} %bitcast.3, f32[1,2048]{1,0:T(1,128)} %gain_hbm.1, bf16[1,2048,896]{2,1,0:T(8,128)(2,1)} %gate_hbm.1, bf16[1,2048,896]{2,1,0:T(8,128)(2,1)} %up_hbm.1, bf16[1,896,2048]{2,1,0:T(8,128)(2,1)} %down_hbm.1), custom_call_target="tpu_custom_call" | custom-call | tf_op jit(solution)/shard_map/expanded_step/pallas_call | solution.py:652
  109.4 0.9 copy.8
